TPU v7x, 512 devices: a whole 4x4x16 slice. The times are simulated.
512 devices in a mesh: row: 32 (over z, core), col: 16 (over x, y).
Axes of the slice: x: 4, y: 4, z: 16, core: 2. Of those that a mesh axis runs over, the one named last changes fastest.
Arguments:
- stiff_tiles: bfloat16 [32, 16, 32, 128, 128], P('row', 'col'), may hold values from -3.5 to 3.5
- stiff_rows: int32 [32, 16, 32], P('row', 'col'), may hold values from 0 to 15, as said below
- stiff_cols: int32 [32, 16, 32], P('row', 'col'), may hold values from 0 to 31, as said below
- product_slot: int32 [32, 16, 32, 3], P('row', 'col'), may hold values from 0 to 7
- prolong_tiles: bfloat16 [512, 3, 128, 128], P(('row', 'col')), may hold values from -0.3125 to 0.3125
- coarse_dest: int32 [512, 3, 8], P(('row', 'col')), may hold values from 0 to 1023, as said below
Outputs:
- galerkin_ap: bfloat16 [512, 8, 128, 128], P(('row', 'col'))
- coarse_tiles: float32 [1024, 128, 128], P(('row', 'col'))
Inputs may be any that keep to these rules, and one draw needn't show every extreme that they name: `stiff_rows`: with stiff_cols: no two entries of one device name the same row and column. Each device holds exactly 2 entries u with u = o, for every o below 16. `stiff_cols`: with stiff_rows: no two entries of one device name the same row and column. `coarse_dest`: coarse tile q is owned by device q // 2 in the order r * 16 + c; every entry held by a device names a tile owned by a device with the same index along row. The entries held by one device name the tiles of one owner at most 4 times; in each grid row some owner is named exactly 4 times by every device of that row.
All inputs are finite; a program needn't handle non-finite values.
Results may differ from a plain program's by a relative error of at most 0.017.
Values may be sent and summed in bfloat16 or wider, within the bound.
No kernel may reach another device: no remote copies, remote signals or barrier semaphores. Data moves between devices by JAX's collectives and lax.ppermute only.
A program may use at most 64 MiB of HBM per device.

v0:
```python
import jax
import jax.numpy as jnp
from jax import lax
from jax.sharding import PartitionSpec as P

CTD = 2


highest = lax.Precision.HIGHEST


def on_device(stiff_tiles, stiff_rows, stiff_cols, product_slot, prolong_tiles, coarse_dest):
    tile_set = stiff_tiles[0, 0]
    tile_rows = stiff_rows[0, 0]
    tile_cols = stiff_cols[0, 0]
    tile_slots = product_slot[0, 0]
    tile_count = tile_set.shape[0]
    tile_edge = tile_set.shape[1]
    own_blocks = prolong_tiles.shape[0]
    per_block = prolong_tiles.shape[1]
    slot_count = coarse_dest.shape[2]
    col_count = lax.axis_size("col")
    band_rows = col_count * own_blocks
    target_count = band_rows * slot_count
    panel_rows = lax.all_gather(prolong_tiles, "row", axis=0, tiled=True)
    targets = (tile_rows[:, None] * slot_count + tile_slots).reshape(-1)
    block_total = 2
    block_size = tile_count // block_total
    row_ids = jnp.arange(target_count, dtype=jnp.int32)
    placing = targets[None, :] == row_ids[:, None]
    gathered = jnp.zeros((row_ids.shape[0], tile_edge * tile_edge), jnp.float32)
    for block_index in range(block_total):
        first_tile = block_index * block_size
        picked = jnp.take(panel_rows, tile_cols[first_tile : first_tile + block_size], axis=0)
        products = jnp.einsum(
            "tij,tkjl->tkil",
            tile_set[first_tile : first_tile + block_size],
            picked,
            preferred_element_type=jnp.float32,
        )
        products = products.reshape(block_size * per_block, tile_edge * tile_edge)
        columns = placing[:, first_tile * per_block : (first_tile + block_size) * per_block].astype(
            jnp.float32
        )
        gathered = gathered + jnp.dot(
            columns, products, precision=highest, preferred_element_type=jnp.float32
        )
    summed = lax.psum_scatter(
        gathered.reshape(band_rows, slot_count, tile_edge, tile_edge).astype(jnp.bfloat16),
        "col",
        scatter_dimension=0,
        tiled=True,
    )
    contrib_count = own_blocks * per_block * slot_count
    contributions = jnp.einsum(
        "gkji,gsjl->gksil", prolong_tiles, summed, preferred_element_type=jnp.float32
    )
    contributions = contributions.reshape(contrib_count, tile_edge * tile_edge)
    destination = coarse_dest.reshape(contrib_count)
    owner_col = destination // CTD % col_count
    owner_tile = destination % CTD
    bucket = owner_col * CTD + owner_tile
    merging = (bucket[None, :] == jnp.arange(col_count * CTD, dtype=jnp.int32)[:, None]).astype(
        jnp.float32
    )
    merged = jnp.dot(merging, contributions, precision=highest, preferred_element_type=jnp.float32)
    received = lax.all_to_all(
        merged.reshape(col_count, CTD, tile_edge * tile_edge).astype(jnp.bfloat16),
        "col",
        split_axis=0,
        concat_axis=0,
        tiled=True,
    ).astype(jnp.float32)
    coarse = jnp.sum(received, axis=0)
    return (summed, coarse.reshape(CTD, tile_edge, tile_edge))


def solution(mesh):
    in_specs = (
        P("row", "col", None, None, None),
        P("row", "col", None),
        P("row", "col", None),
        P("row", "col", None, None),
        P(("row", "col"), None, None, None),
        P(("row", "col"), None, None),
    )
    out_specs = (P(("row", "col"), None, None, None), P(("row", "col"), None, None))
    return jax.shard_map(
        on_device, mesh=mesh, in_specs=in_specs, out_specs=out_specs, check_vma=False
    )
```

profile of v0, /device:TPU:64, one launch (start us, length us, event | category | flops | bytes accessed | tf_op | source)
XLA Modules:
  0.0 244.7 jit_solution(13303089177509714367)
XLA Ops:
  7.2 0.7 all-gather.2.cloned.1.call-update
  8.0 0.7 multiply_bitcast_fusion
  8.8 0.8 copy.21
  9.7 0.8 compare_and_fusion
  10.5 75.4 %all-gather.2.cloned.1.call-done = bf16[32,3,128,128]{3,2,1,0:T(8,128)(2,1)} async-done(((bf16[1,3,128,128]{3,2,1,0:T(8,128)(2,1)}), bf16[32,3,128,128]{3,2,1,0:T(8,128)(2,1)}) %all-gather.2.cloned.1.call-update) | async-done | bytes 3145744 | tf_op jit(solution)/shard_map/all_gather | solution.py:25
  85.9 2.7 %gather_fusion = bf16[16,3,128,128]{3,2,1,0:T(8,128)(2,1)S(1)} fusion(bf16[32,3,128,128]{3,2,1,0:T(8,128)(2,1)} %all-gather.2.cloned.1.call-done, s32[1024]{0:T(1024)S(1)} %get-tuple-element.10), kind=kCustom, calls=%fused_computation.clone | custom fusion | bytes 3145792 | tf_op jit(solution)/shard_map/jit(_take)/gather | solution.py:34
  88.7 2.4 convolution_bitcast_fusion.1
  91.0 2.4 copy.23
  93.4 3.8 %gather_fusion.1 = bf16[16,3,128,128]{3,2,1,0:T(8,128)(2,1)} fusion(bf16[32,3,128,128]{3,2,1,0:T(8,128)(2,1)} %all-gather.2.cloned.1.call-done, s32[1024]{0:T(1024)S(1)} %get-tuple-element.9), kind=kCustom, calls=%fused_computation.1.clone | custom fusion | bytes 3145792 | tf_op jit(solution)/shard_map/jit(_take)/gather | solution.py:34
  97.2 3.9 %convolution_bitcast_fusion = f32[16,3,128,128]{2,3,1,0:T(8,128)} fusion(bf16[16,3,128,128]{3,2,1,0:T(8,128)(2,1)} %gather_fusion.1, pred[16]{0:T(512)(128)(4,1)S(1)} %get-tuple-element.3, bf16[1,1,32,128,128]{4,3,2,1,0:T(8,128)(2,1)} %param.8), kind=kOutput, calls=%fused_computation.12 | convolution fusion | flops 202113024 | bytes 5242896 | tf_op jit(solution)/shard_map/tij,tkjl->tkil/dot_general | solution.py:35
  101.1 3.5 %copy.25 = f32[16,3,128,128]{3,2,1,0:T(8,128)} copy(f32[16,3,128,128]{2,3,1,0:T(8,128)} %convolution_bitcast_fusion) | data formatting | bytes 6291456 | tf_op jit(solution)/shard_map/tij,tkjl->tkil/transpose | solution.py:35
  104.6 5.5 %fusion.3 = f32[128,16384]{1,0:T(8,128)S(1)} fusion(f32[6,8,128,128]{3,2,1,0:T(8,128)S(1)} %bitcast.65, pred[128,96]{1,0:T(32,128)(4,1)S(1)} %iota_compare_fusion), kind=kOutput, calls=%fused_computation.7 | convolution fusion | flops 1207959552 | bytes 11546624 | tf_op jit(solution)/shard_map/dot_general | solution.py:45
  110.1 7.3 %fusion.6 = bf16[16,8,128,128]{3,1,2,0:T(8,128)(2,1)S(1)} fusion(f32[128,16384]{1,0:T(8,128)S(1)} %fusion.3, f32[6,8,128,128]{3,2,1,0:T(8,128)S(1)} %bitcast.66, pred[128,96]{1,0:T(32,128)(4,1)S(1)} %iota_compare_fusion), kind=kOutput, calls=%fused_computation.10 | convolution fusion | flops 1212153856 | bytes 15740928 | tf_op jit(solution)/shard_map/dot_general | solution.py:45
  117.3 3.2 %copy.26 = bf16[16,8,128,128]{3,2,1,0:T(8,128)(2,1)} copy(bf16[16,8,128,128]{3,1,2,0:T(8,128)(2,1)S(1)} %fusion.6) | data formatting | bytes 8388608 | tf_op jit(solution)/shard_map/convert_element_type | solution.py:49
  120.5 0.7 copy-done.3
  121.3 90.4 %reduce-scatter.4.cloned.1.call-done = bf16[1,8,128,128]{3,2,1,0:T(8,128)(2,1)} async-done(((bf16[16,8,128,128]{3,2,1,0:T(8,128)(2,1)}), bf16[1,8,128,128]{3,2,1,0:T(8,128)(2,1)}) %reduce-scatter.4.cloned.1.call-update) | async-done | bytes 262160
  211.8 1.3 convolution_bitcast_fusion.2
  213.1 0.5 copy.28
  213.6 0.3 reshape.170
  213.9 1.0 convolution_convert_fusion
  214.9 1.1 copy.29
  216.0 20.2 %all_to_all.5 = bf16[16,2,16384]{2,1,0:T(2,128)(2,1)S(1)} all-to-all(bf16[16,2,16384]{2,1,0:T(2,128)(2,1)S(1)} %copy.29), channel_id=1, replica_groups=mesh['row'=32,'col'=16] {'col'}, dimensions={0} | all-to-all | bytes 2097152 | tf_op jit(solution)/shard_map/all_to_all | solution.py:67
  236.3 0.9 convert_reduce_fusion
  237.2 0.7 copy.51
  (20 shorter events, 0.5 us)
Async XLA Ops:
  7.2 81.5 %copy-start.1 = (bf16[1,1,32,128,128]{4,3,2,1,0:T(8,128)(2,1)S(1)}, bf16[1,1,32,128,128]{4,3,2,1,0:T(8,128)(2,1)}, u32[]{:S(2)}) copy-start(bf16[1,1,32,128,128]{4,3,2,1,0:T(8,128)(2,1)} %param.8) | copy-start | bytes 3145732
  7.2 78.7 %all-gather.2.cloned.1.call-start = ((), (), s32[]{:S(2)}) async-start(), calls=%async_computation.2 | async-start | bytes 3244032 | tf_op jit(solution)/shard_map/all_gather | solution.py:25
  7.9 203.9 %reduce-scatter.4.cloned.1.call-start = ((), (), s32[]{:S(2)}) async-start(), calls=%async_computation.3 | async-start | bytes 4456448
  104.6 5.5 %copy-start = (f32[16,3,128,128]{3,2,1,0:T(8,128)S(1)}, f32[16,3,128,128]{3,2,1,0:T(8,128)}, u32[]{:S(2)}) copy-start(f32[16,3,128,128]{3,2,1,0:T(8,128)} %copy.25) | copy-start | bytes 9437188
  120.5 0.7 copy-start.3
  120.5 91.3 %copy-start.2 = (bf16[1,3,128,128]{3,2,1,0:T(8,128)(2,1)S(1)}, bf16[1,3,128,128]{3,2,1,0:T(8,128)(2,1)}, u32[]{:S(2)}) copy-start(bf16[1,3,128,128]{3,2,1,0:T(8,128)(2,1)} %param.12) | copy-start | bytes 294916
Sparse Core Ops, SparseCore 0:
  10.1 75.7 all-gather.1
  120.7 91.0 reduce-scatter.3
where the time goes:
time: 245 us
  waiting for transfers between devices  167 us (68%)
  matrix products  21.3 us (9%)
  blocking collectives  20.2 us (8%)
  local copies, waits for them, and re-layouts  19.9 us (8%)
  between operations  14.2 us (6%)
  other arithmetic  2.45 us (1%)
    unnamed x3, waiting for transfers between devices  91.1 us
    all_gather x1, waiting for transfers between devices, on_device(): panel_rows = lax.all_gather(prolong_tiles, 'row', axis=0, tiled=True)  75.4 us
    all_to_all x1, blocking collectives, on_device(): lax.all_to_all(merged.reshape(col_count, CTD, tile_edge * tile_edge).asty...  20.2 us
    dot_general x2, matrix products, on_device(): jnp.dot(columns, products, precision=highest, preferred_element_type=jnp....  12.7 us
    gather x2, local copies, waits for them, and re-layouts, on_device(): jnp.take(panel_rows, tile_cols[first_tile:first_tile + block_size], axis=0)  6.53 us
    dot_general x2, matrix products, on_device(): jnp.einsum('tij,tkjl->tkil', tile_set[first_tile:first_tile + block_size]...  6.22 us
    transpose x2, local copies, waits for them, and re-layouts, on_device(): jnp.einsum('tij,tkjl->tkil', tile_set[first_tile:first_tile + block_size]...  5.91 us
  transfers between devices with their start and end apart: 2, of which 2 were waited for; matrix products, arithmetic and copies ran while one was open for 1% of the time, Pallas kernels for 0%

commit v1 on v0

v1 whole, which is shorter than its diff:
```python
import jax
import jax.numpy as jnp
from jax import lax
from jax.experimental import pallas as pl
from jax.experimental.pallas import tpu as pltpu
from jax.sharding import PartitionSpec as P

TILE = 128
KP = 3
KAP = 8
CTD = 2
COLS = 16
RINGS = 16
ROWS = 2 * RINGS
KA = 32
PAIR = KA // COLS
SHARD = KP * TILE
BODY = PAIR * SHARD
MARK = 16
BLOCK = BODY + MARK
COARSE = COLS * CTD


def product_kernel(
    place_ref, row_ref, slot_ref, tile_ref, *rest
):
    pieces = rest[: len(PIECES)]
    out_ref, panel, marks, count, sems = rest[len(PIECES) :]
    copies = []
    for number, (piece, (first, size)) in enumerate(zip(pieces, PIECES)):
        for k in range(KP):
            copies.append(
                pltpu.make_async_copy(
                    piece.at[:, k],
                    panel.at[pl.ds(first, size), :, pl.ds(k * TILE, TILE)],
                    sems.at[number * KP + k],
                )
            )
    for copy in copies:
        copy.start()
    for owner in range(COLS):
        count[owner] = 0
    marks[...] = jnp.zeros_like(marks)
    lane = lax.broadcasted_iota(jnp.int32, (MARK, TILE), 1)
    for copy in copies:
        copy.wait()
    for t in range(KA):
        owner = row_ref[t]
        which = count[owner]
        count[owner] = which + 1
        product = jnp.dot(
            tile_ref[t], panel[place_ref[t]], preferred_element_type=jnp.float32
        ).astype(jnp.bfloat16)
        for k in range(KP):
            start = pl.multiple_of(which * SHARD + k * TILE, TILE)
            out_ref[owner, pl.ds(start, TILE), :] = product[:, k * TILE : (k + 1) * TILE]
        mark = jnp.zeros((MARK, TILE), jnp.float32)
        for k in range(KP):
            value = slot_ref[t * KP + k].astype(jnp.float32)
            mark = jnp.where(lane == which * KP + k, value, mark)
        marks[owner] = marks[owner] + mark
    out_ref[:, BODY:, :] = marks[...].astype(jnp.bfloat16)


def coarse_kernel(
    bucket_ref, prolong_ref, got_ref, ap_ref, out_ref,
    held, mark_held, mark_int, mark_scalar, total, merged, sems, mark_sems,
):
    chunk_total = held.shape[0]
    chunk = COLS // chunk_total
    mark_copy = pltpu.make_async_copy(got_ref.at[:, pl.ds(BODY, MARK), :], mark_held, mark_sems.at[0])
    mark_copy.start()
    copies = [
        pltpu.make_async_copy(
            got_ref.at[pl.ds(index * chunk, chunk), pl.ds(0, BODY), :], held.at[index], sems.at[index]
        )
        for index in range(chunk_total)
    ]
    for copy in copies:
        copy.start()
    mark_copy.wait()
    mark_int[...] = mark_held[...].astype(jnp.float32)[:, 0, :].astype(jnp.int32)
    scalar_copy = pltpu.make_async_copy(mark_int, mark_scalar, mark_sems.at[1])
    scalar_copy.start()
    total[...] = jnp.zeros_like(total)
    merged[...] = jnp.zeros_like(merged)
    scalar_copy.wait()
    for index in range(chunk_total):
        copies[index].wait()
        for peer in range(chunk):
            for q in range(PAIR * KP):
                slot = mark_scalar[index * chunk + peer, q]
                total[slot] = total[slot] + held[index, peer, pl.ds(q * TILE, TILE), :].astype(jnp.float32)
    for s in range(KAP):
        ap = total[s].astype(jnp.bfloat16)
        ap_ref[s] = ap
        for k in range(KP):
            term = lax.dot_general(
                prolong_ref[k], ap, (((0,), (0,)), ((), ())), preferred_element_type=jnp.float32
            )
            bucket = bucket_ref[k * KAP + s]
            merged[bucket] = merged[bucket] + term
    out_ref[...] = merged[...].astype(jnp.bfloat16)


PIECES = ((0, 4), (4, 4), (8, 4), (12, 2), (14, 2), (16, 4), (20, 4), (24, 4), (28, 2), (30, 2))


def shifted(array, step):
    pairs = [
        (2 * z + core, 2 * ((z + step) % RINGS) + core) for z in range(RINGS) for core in range(2)
    ]
    return lax.ppermute(array, "row", pairs)


def to_sibling(array):
    return lax.ppermute(array, "row", [(r, r ^ 1) for r in range(ROWS)])


def gather_pieces(prolong):
    own = prolong.reshape(SHARD, TILE)
    half = SHARD // 2
    below = shifted(own, 4)
    above = shifted(own, -4)
    first = shifted(above[:half], -4)
    second = shifted(below[half:], 4)
    own4 = jnp.concatenate([own, below, first, second, above])
    prev4 = shifted(own4, 1)
    next4 = shifted(own4, -1)
    far_next = shifted(next4[: 2 * SHARD], -1)
    far_prev = shifted(prev4[SHARD : 3 * SHARD], 1)
    mine = [own4, prev4, next4, far_next, far_prev]
    pieces = mine + [to_sibling(piece) for piece in mine]
    return [piece.reshape(-1, KP, TILE, TILE) for piece in pieces]


def panel_place(tile_cols):
    row = lax.axis_index("row")
    delta = (tile_cols // 2 - row // 2) % RINGS
    kind = delta % 4
    base = jnp.where(kind == 0, 0, jnp.where(kind == 3, 4, jnp.where(kind == 1, 8, 12)))
    offset = jnp.where(kind == 3, -1, kind)
    index = ((offset - delta + 2 * RINGS) // 4) % 4
    return base + index + jnp.where(tile_cols % 2 == row % 2, 0, RINGS)


def on_device(stiff_tiles, stiff_rows, stiff_cols, product_slot, prolong_tiles, coarse_dest):
    scalars = pl.BlockSpec(memory_space=pltpu.SMEM)
    vmem = pl.BlockSpec(memory_space=pltpu.VMEM)
    anywhere = pl.BlockSpec(memory_space=pl.ANY)
    prolong = prolong_tiles[0]
    pieces = gather_pieces(prolong)
    place = panel_place(stiff_cols[0, 0])
    sent = pl.pallas_call(
        product_kernel,
        out_shape=jax.ShapeDtypeStruct((COLS, BLOCK, TILE), jnp.bfloat16),
        in_specs=[scalars] * 3 + [vmem] + [anywhere] * len(PIECES),
        out_specs=vmem,
        scratch_shapes=[
            pltpu.VMEM((ROWS, TILE, SHARD), jnp.bfloat16),
            pltpu.VMEM((COLS, MARK, TILE), jnp.float32),
            pltpu.SMEM((COLS,), jnp.int32),
            pltpu.SemaphoreType.DMA((len(PIECES) * KP,)),
        ],
        compiler_params=pltpu.CompilerParams(vmem_limit_bytes=24 * 2**20),
    )(place, stiff_rows[0, 0], product_slot[0, 0].reshape(KA * KP), stiff_tiles[0, 0], *pieces)
    got = lax.all_to_all(sent, "col", split_axis=0, concat_axis=0, tiled=True)
    chunk_total = 4
    ap, merged = pl.pallas_call(
        coarse_kernel,
        out_shape=(
            jax.ShapeDtypeStruct((KAP, TILE, TILE), jnp.bfloat16),
            jax.ShapeDtypeStruct((COARSE, TILE, TILE), jnp.bfloat16),
        ),
        in_specs=[scalars, vmem, anywhere],
        out_specs=(vmem, vmem),
        scratch_shapes=[
            pltpu.VMEM((chunk_total, COLS // chunk_total, BODY, TILE), jnp.bfloat16),
            pltpu.VMEM((COLS, MARK, TILE), jnp.bfloat16),
            pltpu.VMEM((COLS, TILE), jnp.int32),
            pltpu.SMEM((COLS, TILE), jnp.int32),
            pltpu.VMEM((KAP, TILE, TILE), jnp.float32),
            pltpu.VMEM((COARSE, TILE, TILE), jnp.float32),
            pltpu.SemaphoreType.DMA((chunk_total,)),
            pltpu.SemaphoreType.DMA((2,)),
        ],
        compiler_params=pltpu.CompilerParams(vmem_limit_bytes=24 * 2**20),
    )(coarse_dest.reshape(KP * KAP) % COARSE, prolong, got)
    received = lax.all_to_all(merged, "col", split_axis=0, concat_axis=0, tiled=True)
    coarse = jnp.sum(received.reshape(COLS, CTD, TILE, TILE).astype(jnp.float32), axis=0)
    return (ap[None], coarse)


def solution(mesh):
    in_specs = (
        P("row", "col", None, None, None),
        P("row", "col", None),
        P("row", "col", None),
        P("row", "col", None, None),
        P(("row", "col"), None, None, None),
        P(("row", "col"), None, None),
    )
    out_specs = (P(("row", "col"), None, None, None), P(("row", "col"), None, None))
    return jax.shard_map(
        on_device, mesh=mesh, in_specs=in_specs, out_specs=out_specs, check_vma=False
    )
```

time: 245 us -> 162 us (0.66)
  the two profiles are of different devices: /device:TPU:64 before, /device:TPU:96 now
where the time goes in v1:
time: 162 us; the launch traced here: 161 us
  waiting for transfers between devices  63.6 us (39%)
  starting transfers between devices  56.7 us (35%)
  blocking collectives  26.7 us (16%)
  Pallas kernels  6.08 us (4%)
  local copies, waits for them, and re-layouts  5.49 us (3%)
    all_to_all x1, waiting for transfers between devices, on_device(): got = lax.all_to_all(sent, 'col', split_axis=0, concat_axis=0, tiled=True)  43.2 us
    ppermute x8, starting transfers between devices, shifted(): return lax.ppermute(array, 'row', pairs)  39 us
    all_to_all x1, blocking collectives, on_device(): lax.all_to_all(merged, 'col', split_axis=0, concat_axis=0, tiled=True)  26.7 us
    ppermute x8, waiting for transfers between devices, shifted(): return lax.ppermute(array, 'row', pairs)  19.7 us
    ppermute x5, starting transfers between devices, to_sibling(): return lax.ppermute(array, 'row', [(r, r ^ 1) for r in range(ROWS)])  10.6 us
    all_to_all x1, starting transfers between devices, on_device(): got = lax.all_to_all(sent, 'col', split_axis=0, concat_axis=0, tiled=True)  7.21 us
    unnamed x15, local copies, waits for them, and re-layouts  5.25 us
    pallas_call x1, Pallas kernels, on_device(): pl.pallas_call(coarse_kernel, out_shape=(jax.ShapeDtypeStruct((KAP, TILE,...  3.48 us
  transfers between devices with their start and end apart: 14, of which 6 were waited for; matrix products, arithmetic and copies ran while one was open for 2% of the time, Pallas kernels for 0%

profile of v1, /device:TPU:96, one launch (start us, length us, event | category | flops | bytes accessed | tf_op | source)
XLA Modules:
  0.0 161.0 jit_solution(17775645655051454276)
XLA Ops:
  0.6 9.1 %collective-permute-start = (bf16[384,128]{1,0:T(8,128)(2,1)}, bf16[384,128]{1,0:T(8,128)(2,1)S(1)}, u32[]{:S(2)}, u32[]{:S(2)}) collective-permute-start(bf16[384,128]{1,0:T(8,128)(2,1)} %bitcast.36), channel_id=1, source_target_pairs={{0,128},{16,144},{32,160},{48,176},{64,192},{80,208},{96,224},{112... | collective-permute-start | bytes 294920 | tf_op jit(solution)/shard_map/ppermute | solution.py:113
  9.7 2.9 %collective-permute-start.1 = (bf16[384,128]{1,0:T(8,128)(2,1)}, bf16[384,128]{1,0:T(8,128)(2,1)S(1)}, u32[]{:S(2)}, u32[]{:S(2)}) collective-permute-start(bf16[384,128]{1,0:T(8,128)(2,1)} %bitcast.37), channel_id=1, source_target_pairs={{0,384},{16,400},{32,416},{48,432},{64,448},{80,464},{96,480},{112... | collective-permute-start | bytes 294920 | tf_op jit(solution)/shard_map/ppermute | solution.py:113
  12.6 0.9 constant_dynamic-update-slice_fusion.4
  13.5 7.0 %collective-permute-done.1 = bf16[384,128]{1,0:T(8,128)(2,1)S(1)} collective-permute-done((bf16[384,128]{1,0:T(8,128)(2,1)}, bf16[384,128]{1,0:T(8,128)(2,1)S(1)}, u32[]{:S(2)}, u32[]{:S(2)}) %collective-permute-start.1) | collective-permute-done | bytes 98336 | tf_op jit(solution)/shard_map/ppermute | solution.py:113
  20.5 7.0 %collective-permute-start.2 = (bf16[192,128]{1,0:T(8,128)(2,1)S(1)}, bf16[192,128]{1,0:T(8,128)(2,1)S(1)}, u32[]{:S(2)}, u32[]{:S(2)}) collective-permute-start(bf16[192,128]{1,0:T(8,128)(2,1)S(1)} %slice.16), channel_id=1, source_target_pairs={{0,384},{16,400},{32,416},{48,432},{64,448},{80,464},{96,480},{112... | collective-permute-start | bytes 147464 | tf_op jit(solution)/shard_map/ppermute | solution.py:113
  27.6 5.2 %collective-permute-start.3 = (bf16[192,128]{1,0:T(8,128)(2,1)S(1)}, bf16[192,128]{1,0:T(8,128)(2,1)S(1)}, u32[]{:S(2)}, u32[]{:S(2)}) collective-permute-start(bf16[192,128]{1,0:T(8,128)(2,1)S(1)} %slice.17), channel_id=1, source_target_pairs={{0,128},{16,144},{32,160},{48,176},{64,192},{80,208},{96,224},{112... | collective-permute-start | bytes 147464 | tf_op jit(solution)/shard_map/ppermute | solution.py:113
  33.0 5.3 %collective-permute-done.3 = bf16[192,128]{1,0:T(8,128)(2,1)S(1)} collective-permute-done((bf16[192,128]{1,0:T(8,128)(2,1)S(1)}, bf16[192,128]{1,0:T(8,128)(2,1)S(1)}, u32[]{:S(2)}, u32[]{:S(2)}) %collective-permute-start.3) | collective-permute-done | bytes 49184 | tf_op jit(solution)/shard_map/ppermute | solution.py:113
  38.3 2.0 %collective-permute-start.5 = (bf16[1536,128]{1,0:T(8,128)(2,1)S(1)}, bf16[1536,128]{1,0:T(8,128)(2,1)S(1)}, u32[]{:S(2)}, u32[]{:S(2)}) collective-permute-start(bf16[1536,128]{1,0:T(8,128)(2,1)S(1)} %constant_dynamic-update-slice_fusion), channel_id=1, source_target_pairs={{0,480},{16,496},{32,0},{48,16},{64,32},{80,48},{96,64},{112,80},{... | collective-permute-start | bytes 1179656 | tf_op jit(solution)/shard_map/ppermute | solution.py:113
  40.3 5.7 %collective-permute-start.4 = (bf16[1536,128]{1,0:T(8,128)(2,1)S(1)}, bf16[1536,128]{1,0:T(8,128)(2,1)S(1)}, u32[]{:S(2)}, u32[]{:S(2)}) collective-permute-start(bf16[1536,128]{1,0:T(8,128)(2,1)S(1)} %constant_dynamic-update-slice_fusion), channel_id=1, source_target_pairs={{0,32},{16,48},{32,64},{48,80},{64,96},{80,112},{96,128},{112,144}... | collective-permute-start | bytes 1179656 | tf_op jit(solution)/shard_map/ppermute | solution.py:113
  46.0 7.3 %collective-permute-done.5 = bf16[1536,128]{1,0:T(8,128)(2,1)S(1)} collective-permute-done((bf16[1536,128]{1,0:T(8,128)(2,1)S(1)}, bf16[1536,128]{1,0:T(8,128)(2,1)S(1)}, u32[]{:S(2)}, u32[]{:S(2)}) %collective-permute-start.5) | collective-permute-done | bytes 393248 | tf_op jit(solution)/shard_map/ppermute | solution.py:113
  53.3 1.9 %collective-permute-start.6 = (bf16[768,128]{1,0:T(8,128)(2,1)S(1)}, bf16[768,128]{1,0:T(8,128)(2,1)S(1)}, u32[]{:S(2)}, u32[]{:S(2)}) collective-permute-start(bf16[768,128]{1,0:T(8,128)(2,1)S(1)} %slice.18), channel_id=1, source_target_pairs={{0,480},{16,496},{32,0},{48,16},{64,32},{80,48},{96,64},{112,80},{... | collective-permute-start | bytes 589832 | tf_op jit(solution)/shard_map/ppermute | solution.py:113
  55.3 5.1 %collective-permute-start.7 = (bf16[768,128]{1,0:T(8,128)(2,1)S(1)}, bf16[768,128]{1,0:T(8,128)(2,1)S(1)}, u32[]{:S(2)}, u32[]{:S(2)}) collective-permute-start(bf16[768,128]{1,0:T(8,128)(2,1)S(1)} %slice.19), channel_id=1, source_target_pairs={{0,32},{16,48},{32,64},{48,80},{64,96},{80,112},{96,128},{112,144}... | collective-permute-start | bytes 589832 | tf_op jit(solution)/shard_map/ppermute | solution.py:113
  60.4 1.9 %collective-permute-start.8 = (bf16[1536,128]{1,0:T(8,128)(2,1)S(1)}, bf16[1536,128]{1,0:T(8,128)(2,1)S(1)}, u32[]{:S(2)}, u32[]{:S(2)}) collective-permute-start(bf16[1536,128]{1,0:T(8,128)(2,1)S(1)} %constant_dynamic-update-slice_fusion), channel_id=1, source_target_pairs={{0,16},{16,0},{32,48},{48,32},{64,80},{80,64},{96,112},{112,96},{1... | collective-permute-start | bytes 1179656 | tf_op jit(solution)/shard_map/ppermute | solution.py:117
  62.4 2.4 %collective-permute-start.9 = (bf16[1536,128]{1,0:T(8,128)(2,1)S(1)}, bf16[1536,128]{1,0:T(8,128)(2,1)S(1)}, u32[]{:S(2)}, u32[]{:S(2)}) collective-permute-start(bf16[1536,128]{1,0:T(8,128)(2,1)S(1)} %collective-permute-done.4), channel_id=1, source_target_pairs={{0,16},{16,0},{32,48},{48,32},{64,80},{80,64},{96,112},{112,96},{1... | collective-permute-start | bytes 1179656 | tf_op jit(solution)/shard_map/ppermute | solution.py:117
  64.8 1.9 %collective-permute-start.10 = (bf16[1536,128]{1,0:T(8,128)(2,1)S(1)}, bf16[1536,128]{1,0:T(8,128)(2,1)S(1)}, u32[]{:S(2)}, u32[]{:S(2)}) collective-permute-start(bf16[1536,128]{1,0:T(8,128)(2,1)S(1)} %collective-permute-done.5), channel_id=1, source_target_pairs={{0,16},{16,0},{32,48},{48,32},{64,80},{80,64},{96,112},{112,96},{1... | collective-permute-start | bytes 1179656 | tf_op jit(solution)/shard_map/ppermute | solution.py:117
  67.6 2.4 %collective-permute-start.11 = (bf16[768,128]{1,0:T(8,128)(2,1)S(1)}, bf16[768,128]{1,0:T(8,128)(2,1)S(1)}, u32[]{:S(2)}, u32[]{:S(2)}) collective-permute-start(bf16[768,128]{1,0:T(8,128)(2,1)S(1)} %collective-permute-done.6), channel_id=1, source_target_pairs={{0,16},{16,0},{32,48},{48,32},{64,80},{80,64},{96,112},{112,96},{1... | collective-permute-start | bytes 589832 | tf_op jit(solution)/shard_map/ppermute | solution.py:117
  70.0 1.9 %collective-permute-start.12 = (bf16[768,128]{1,0:T(8,128)(2,1)S(1)}, bf16[768,128]{1,0:T(8,128)(2,1)S(1)}, u32[]{:S(2)}, u32[]{:S(2)}) collective-permute-start(bf16[768,128]{1,0:T(8,128)(2,1)S(1)} %collective-permute-done.7), channel_id=1, source_target_pairs={{0,16},{16,0},{32,48},{48,32},{64,80},{80,64},{96,112},{112,96},{1... | collective-permute-start | bytes 589832 | tf_op jit(solution)/shard_map/ppermute | solution.py:117
  73.4 1.2 copy-done.1
  75.3 2.6 %shard_map.77 = bf16[16,784,128]{2,1,0:T(8,128)(2,1)S(1)} custom-call(s32[32]{0:T(128)S(1)} %fusion.1.place_ref, s32[32]{0:T(128)S(1)} %bitcast.47, s32[96]{0:T(128)S(1)} %reshape_squeeze.6.slot_ref, bf16[32,128,128]{2,1,0:T(8,128)(2,1)S(1)} %bitcast.32, bf16[4,3,128,128]{3,2,1,0:T(8,128)(2,1)S(1)} %bitcast.35, bf16[4,3,128,128]{3,2,1,0:T(8,128)(2,1)S(1)} %bitcast.34, ...), custom_call_target="tpu_custom_call" | custom-call | tf_op jit(solution)/shard_map/pallas_call | solution.py:154
  77.9 1.7 %copy-done = bf16[16,784,128]{2,1,0:T(8,128)(2,1)} copy-done((bf16[16,784,128]{2,1,0:T(8,128)(2,1)}, bf16[16,784,128]{2,1,0:T(8,128)(2,1)S(1)}, u32[]{:S(2)}) %copy-start) | copy-done | bytes 3211288
  79.6 7.2 %all-to-all-start = ((bf16[16,784,128]{2,1,0:T(8,128)(2,1)}), bf16[16,784,128]{2,1,0:T(8,128)(2,1)S(1)}, u32[]{:S(2)}, u32[]{:S(2)}) async-start(bf16[16,784,128]{2,1,0:T(8,128)(2,1)} %copy-done), calls=%async_computation | async-start | bytes 6422528 | tf_op jit(solution)/shard_map/all_to_all | solution.py:167
  86.9 43.2 %all-to-all-done.got_ref = bf16[16,784,128]{2,1,0:T(8,128)(2,1)S(1)} async-done(((bf16[16,784,128]{2,1,0:T(8,128)(2,1)}), bf16[16,784,128]{2,1,0:T(8,128)(2,1)S(1)}, u32[]{:S(2)}, u32[]{:S(2)}) %all-to-all-start) | async-done | bytes 3211296 | tf_op jit(solution)/shard_map/all_to_all | solution.py:167
  130.1 3.5 %shard_map.78 = (bf16[8,128,128]{2,1,0:T(8,128)(2,1)}, bf16[32,128,128]{2,1,0:T(8,128)(2,1)S(1)}) custom-call(s32[24]{0:T(128)S(1)} %and_select_fusion.6.bucket_ref, bf16[3,128,128]{2,1,0:T(8,128)(2,1)S(1)} %bitcast.39, bf16[16,784,128]{2,1,0:T(8,128)(2,1)S(1)} %all-to-all-done.got_ref), custom_call_target="tpu_custom_call" | custom-call | tf_op jit(solution)/shard_map/pallas_call | solution.py:169
  133.5 26.7 %all_to_all.10 = bf16[32,128,128]{2,1,0:T(8,128)(2,1)S(1)} all-to-all(bf16[32,128,128]{2,1,0:T(8,128)(2,1)S(1)} %get-tuple-element.5), channel_id=1, replica_groups=mesh['row'=32,'col'=16] {'col'}, dimensions={0} | all-to-all | bytes 2097152 | tf_op jit(solution)/shard_map/all_to_all | solution.py:189
  (33 shorter events, 4.1 us)
Async XLA Ops:
  0.6 26.9 %collective-permute-start = (bf16[384,128]{1,0:T(8,128)(2,1)}, bf16[384,128]{1,0:T(8,128)(2,1)S(1)}, u32[]{:S(2)}, u32[]{:S(2)}) collective-permute-start(bf16[384,128]{1,0:T(8,128)(2,1)} %bitcast.36), channel_id=1, source_target_pairs={{0,128},{16,144},{32,160},{48,176},{64,192},{80,208},{96,224},{112... | collective-permute-start | bytes 294920 | tf_op jit(solution)/shard_map/ppermute | solution.py:113
  9.7 10.8 %collective-permute-start.1 = (bf16[384,128]{1,0:T(8,128)(2,1)}, bf16[384,128]{1,0:T(8,128)(2,1)S(1)}, u32[]{:S(2)}, u32[]{:S(2)}) collective-permute-start(bf16[384,128]{1,0:T(8,128)(2,1)} %bitcast.37), channel_id=1, source_target_pairs={{0,384},{16,400},{32,416},{48,432},{64,448},{80,464},{96,480},{112... | collective-permute-start | bytes 294920 | tf_op jit(solution)/shard_map/ppermute | solution.py:113
  20.5 12.4 %collective-permute-start.2 = (bf16[192,128]{1,0:T(8,128)(2,1)S(1)}, bf16[192,128]{1,0:T(8,128)(2,1)S(1)}, u32[]{:S(2)}, u32[]{:S(2)}) collective-permute-start(bf16[192,128]{1,0:T(8,128)(2,1)S(1)} %slice.16), channel_id=1, source_target_pairs={{0,384},{16,400},{32,416},{48,432},{64,448},{80,464},{96,480},{112... | collective-permute-start | bytes 147464 | tf_op jit(solution)/shard_map/ppermute | solution.py:113
  27.6 10.7 %collective-permute-start.3 = (bf16[192,128]{1,0:T(8,128)(2,1)S(1)}, bf16[192,128]{1,0:T(8,128)(2,1)S(1)}, u32[]{:S(2)}, u32[]{:S(2)}) collective-permute-start(bf16[192,128]{1,0:T(8,128)(2,1)S(1)} %slice.17), channel_id=1, source_target_pairs={{0,128},{16,144},{32,160},{48,176},{64,192},{80,208},{96,224},{112... | collective-permute-start | bytes 147464 | tf_op jit(solution)/shard_map/ppermute | solution.py:113
  38.3 15.0 %collective-permute-start.5 = (bf16[1536,128]{1,0:T(8,128)(2,1)S(1)}, bf16[1536,128]{1,0:T(8,128)(2,1)S(1)}, u32[]{:S(2)}, u32[]{:S(2)}) collective-permute-start(bf16[1536,128]{1,0:T(8,128)(2,1)S(1)} %constant_dynamic-update-slice_fusion), channel_id=1, source_target_pairs={{0,480},{16,496},{32,0},{48,16},{64,32},{80,48},{96,64},{112,80},{... | collective-permute-start | bytes 1179656 | tf_op jit(solution)/shard_map/ppermute | solution.py:113
  40.3 15.0 %collective-permute-start.4 = (bf16[1536,128]{1,0:T(8,128)(2,1)S(1)}, bf16[1536,128]{1,0:T(8,128)(2,1)S(1)}, u32[]{:S(2)}, u32[]{:S(2)}) collective-permute-start(bf16[1536,128]{1,0:T(8,128)(2,1)S(1)} %constant_dynamic-update-slice_fusion), channel_id=1, source_target_pairs={{0,32},{16,48},{32,64},{48,80},{64,96},{80,112},{96,128},{112,144}... | collective-permute-start | bytes 1179656 | tf_op jit(solution)/shard_map/ppermute | solution.py:113
  53.3 14.3 %collective-permute-start.6 = (bf16[768,128]{1,0:T(8,128)(2,1)S(1)}, bf16[768,128]{1,0:T(8,128)(2,1)S(1)}, u32[]{:S(2)}, u32[]{:S(2)}) collective-permute-start(bf16[768,128]{1,0:T(8,128)(2,1)S(1)} %slice.18), channel_id=1, source_target_pairs={{0,480},{16,496},{32,0},{48,16},{64,32},{80,48},{96,64},{112,80},{... | collective-permute-start | bytes 589832 | tf_op jit(solution)/shard_map/ppermute | solution.py:113
  55.3 14.7 %collective-permute-start.7 = (bf16[768,128]{1,0:T(8,128)(2,1)S(1)}, bf16[768,128]{1,0:T(8,128)(2,1)S(1)}, u32[]{:S(2)}, u32[]{:S(2)}) collective-permute-start(bf16[768,128]{1,0:T(8,128)(2,1)S(1)} %slice.19), channel_id=1, source_target_pairs={{0,32},{16,48},{32,64},{48,80},{64,96},{80,112},{96,128},{112,144}... | collective-permute-start | bytes 589832 | tf_op jit(solution)/shard_map/ppermute | solution.py:113
  60.4 12.2 %collective-permute-start.8 = (bf16[1536,128]{1,0:T(8,128)(2,1)S(1)}, bf16[1536,128]{1,0:T(8,128)(2,1)S(1)}, u32[]{:S(2)}, u32[]{:S(2)}) collective-permute-start(bf16[1536,128]{1,0:T(8,128)(2,1)S(1)} %constant_dynamic-update-slice_fusion), channel_id=1, source_target_pairs={{0,16},{16,0},{32,48},{48,32},{64,80},{80,64},{96,112},{112,96},{1... | collective-permute-start | bytes 1179656 | tf_op jit(solution)/shard_map/ppermute | solution.py:117
  62.4 11.0 %collective-permute-start.9 = (bf16[1536,128]{1,0:T(8,128)(2,1)S(1)}, bf16[1536,128]{1,0:T(8,128)(2,1)S(1)}, u32[]{:S(2)}, u32[]{:S(2)}) collective-permute-start(bf16[1536,128]{1,0:T(8,128)(2,1)S(1)} %collective-permute-done.4), channel_id=1, source_target_pairs={{0,16},{16,0},{32,48},{48,32},{64,80},{80,64},{96,112},{112,96},{1... | collective-permute-start | bytes 1179656 | tf_op jit(solution)/shard_map/ppermute | solution.py:117
  64.8 8.6 %collective-permute-start.10 = (bf16[1536,128]{1,0:T(8,128)(2,1)S(1)}, bf16[1536,128]{1,0:T(8,128)(2,1)S(1)}, u32[]{:S(2)}, u32[]{:S(2)}) collective-permute-start(bf16[1536,128]{1,0:T(8,128)(2,1)S(1)} %collective-permute-done.5), channel_id=1, source_target_pairs={{0,16},{16,0},{32,48},{48,32},{64,80},{80,64},{96,112},{112,96},{1... | collective-permute-start | bytes 1179656 | tf_op jit(solution)/shard_map/ppermute | solution.py:117
  67.6 5.1 %collective-permute-start.11 = (bf16[768,128]{1,0:T(8,128)(2,1)S(1)}, bf16[768,128]{1,0:T(8,128)(2,1)S(1)}, u32[]{:S(2)}, u32[]{:S(2)}) collective-permute-start(bf16[768,128]{1,0:T(8,128)(2,1)S(1)} %collective-permute-done.6), channel_id=1, source_target_pairs={{0,16},{16,0},{32,48},{48,32},{64,80},{80,64},{96,112},{112,96},{1... | collective-permute-start | bytes 589832 | tf_op jit(solution)/shard_map/ppermute | solution.py:117
  70.0 3.3 %collective-permute-start.12 = (bf16[768,128]{1,0:T(8,128)(2,1)S(1)}, bf16[768,128]{1,0:T(8,128)(2,1)S(1)}, u32[]{:S(2)}, u32[]{:S(2)}) collective-permute-start(bf16[768,128]{1,0:T(8,128)(2,1)S(1)} %collective-permute-done.7), channel_id=1, source_target_pairs={{0,16},{16,0},{32,48},{48,32},{64,80},{80,64},{96,112},{112,96},{1... | collective-permute-start | bytes 589832 | tf_op jit(solution)/shard_map/ppermute | solution.py:117
  73.4 1.2 copy-start.1
  74.6 0.7 copy-start.3
  77.9 1.7 %copy-start = (bf16[16,784,128]{2,1,0:T(8,128)(2,1)}, bf16[16,784,128]{2,1,0:T(8,128)(2,1)S(1)}, u32[]{:S(2)}) copy-start(bf16[16,784,128]{2,1,0:T(8,128)(2,1)S(1)} %shard_map.77) | copy-start | bytes 9633796
  79.5 7.2 %copy-start.4 = (s32[1,3,8]{2,0,1:T(1,128)S(1)}, s32[1,3,8]{2,0,1:T(1,128)}, u32[]{:S(2)}) copy-start(s32[1,3,8]{2,0,1:T(1,128)} %param.11) | copy-start | bytes 292
  79.6 50.5 %copy-start.2 = (bf16[1,3,128,128]{3,2,1,0:T(8,128)(2,1)S(1)}, bf16[1,3,128,128]{3,2,1,0:T(8,128)(2,1)}, u32[]{:S(2)}) copy-start(bf16[1,3,128,128]{3,2,1,0:T(8,128)(2,1)} %param.10) | copy-start | bytes 294916
  79.6 50.5 %all-to-all-start = ((bf16[16,784,128]{2,1,0:T(8,128)(2,1)}), bf16[16,784,128]{2,1,0:T(8,128)(2,1)S(1)}, u32[]{:S(2)}, u32[]{:S(2)}) async-start(bf16[16,784,128]{2,1,0:T(8,128)(2,1)} %copy-done), calls=%async_computation | async-start | bytes 6422528 | tf_op jit(solution)/shard_map/all_to_all | solution.py:167

commit v2 on v1

v2 whole, which is shorter than its diff:
```python
import jax
import jax.numpy as jnp
from jax import lax
from jax.experimental import pallas as pl
from jax.experimental.pallas import tpu as pltpu
from jax.sharding import PartitionSpec as P

TILE = 128
KP = 3
KAP = 8
CTD = 2
COLS = 16
RINGS = 16
ROWS = 2 * RINGS
KA = 32
PAIR = KA // COLS
SHARD = KP * TILE
BODY = PAIR * SHARD
MARK = 16
BLOCK = BODY + MARK
COARSE = COLS * CTD
K1_MIB = 57
SPOT = 2 * KA + KA * KP


def product_kernel(scalar_ref, tile_ref, *rest):
    pieces = rest[: len(PIECES)]
    out_ref, panel, tiles, outs, order, count, sems, tile_sem, out_sems = rest[len(PIECES) :]
    tile_copy = pltpu.make_async_copy(tile_ref, tiles, tile_sem.at[0])
    tile_copy.start()
    copies = []
    for number, (piece, (first, size)) in enumerate(zip(pieces, PIECES)):
        for k in range(KP):
            copies.append(
                pltpu.make_async_copy(
                    piece.at[:, k],
                    panel.at[pl.ds(first, size), :, pl.ds(k * TILE, TILE)],
                    sems.at[number * KP + k],
                )
            )
    for copy in copies:
        copy.start()
    for owner in range(COLS):
        count[owner] = 0
    for t in range(KA):
        owner = scalar_ref[KA + t]
        which = count[owner]
        count[owner] = which + 1
        order[owner * PAIR + which] = t
    lane = lax.broadcasted_iota(jnp.int32, (MARK, TILE), 1)
    tile_copy.wait()
    for copy in copies:
        copy.wait()
    out_copies = []
    for owner in range(COLS):
        mark = jnp.zeros((MARK, TILE), jnp.float32)
        for which in range(PAIR):
            t = order[owner * PAIR + which]
            product = jnp.dot(
                tiles[t], panel[scalar_ref[t]], preferred_element_type=jnp.float32
            ).astype(jnp.bfloat16)
            for k in range(KP):
                q = which * KP + k
                outs[owner, q * TILE : (q + 1) * TILE, :] = product[:, k * TILE : (k + 1) * TILE]
                value = scalar_ref[2 * KA + t * KP + k].astype(jnp.float32)
                mark = jnp.where(lane == q, value, mark)
        outs[owner, BODY:, :] = mark.astype(jnp.bfloat16)
        out_copy = pltpu.make_async_copy(outs.at[owner], out_ref.at[owner], out_sems.at[owner])
        out_copy.start()
        out_copies.append(out_copy)
    for out_copy in out_copies:
        out_copy.wait()


def coarse_kernel(
    scalar_ref, prolong_ref, got_ref, ap_ref, out_ref,
    held, mark_held, mark_int, mark_scalar, total, merged, rounded, sems, mark_sems,
):
    chunk_total = held.shape[0]
    chunk = COLS // chunk_total
    mark_copy = pltpu.make_async_copy(got_ref.at[:, pl.ds(BODY, MARK), :], mark_held, mark_sems.at[0])
    mark_copy.start()
    copies = [
        pltpu.make_async_copy(
            got_ref.at[pl.ds(index * chunk, chunk), pl.ds(0, BODY), :], held.at[index], sems.at[index]
        )
        for index in range(chunk_total)
    ]
    for copy in copies:
        copy.start()
    mark_copy.wait()
    mark_int[...] = mark_held[...].astype(jnp.float32)[:, 0, :].astype(jnp.int32)
    scalar_copy = pltpu.make_async_copy(mark_int, mark_scalar, mark_sems.at[1])
    scalar_copy.start()
    total[...] = jnp.zeros_like(total)
    merged[...] = jnp.zeros_like(merged)
    scalar_copy.wait()
    for index in range(chunk_total):
        copies[index].wait()
        for peer in range(chunk):
            for q in range(PAIR * KP):
                slot = mark_scalar[index * chunk + peer, q]
                total[slot] = total[slot] + held[index, peer, pl.ds(q * TILE, TILE), :].astype(jnp.float32)
    for s in range(KAP):
        ap = total[s].astype(jnp.bfloat16)
        ap_ref[s] = ap
        for k in range(KP):
            term = lax.dot_general(
                prolong_ref[k], ap, (((0,), (0,)), ((), ())), preferred_element_type=jnp.float32
            )
            bucket = scalar_ref[SPOT + k * KAP + s]
            merged[bucket] = merged[bucket] + term
    rounded[...] = merged[...].astype(jnp.bfloat16)
    out_copy = pltpu.make_async_copy(rounded, out_ref, mark_sems.at[2])
    out_copy.start()
    out_copy.wait()


PIECES = ((0, 8), (8, 4), (12, 4), (16, 8), (24, 4), (28, 4))


def shifted(array, step):
    pairs = [
        (2 * z + core, 2 * ((z + step) % RINGS) + core) for z in range(RINGS) for core in range(2)
    ]
    return lax.ppermute(array, "row", pairs)


def to_sibling(array):
    return lax.ppermute(array, "row", [(r, r ^ 1) for r in range(ROWS)])


def gather_pieces(prolong, numbers):
    groups = [[2 * (low + 2 * k) + core for k in range(8)] for low in range(2) for core in range(2)]
    own8 = lax.all_gather(
        prolong.reshape(SHARD, TILE), "row", axis=0, tiled=True, axis_index_groups=groups
    )
    other8 = to_sibling(own8)
    low4 = shifted(own8[: 4 * SHARD], 1)
    high4 = shifted(own8[4 * SHARD :], -1)
    low4, high4, numbers = lax.optimization_barrier((low4, high4, numbers))
    pieces = [own8, low4, high4, other8, to_sibling(low4), to_sibling(high4)]
    return [piece.reshape(-1, KP, TILE, TILE) for piece in pieces], numbers


def panel_place(tile_cols):
    row = lax.axis_index("row")
    ring = tile_cols // 2
    return (
        ring // 2
        + jnp.where((ring - row // 2) % 2 == 0, 0, 8)
        + jnp.where((tile_cols - row) % 2 == 0, 0, RINGS)
    )


def on_device(stiff_tiles, stiff_rows, stiff_cols, product_slot, prolong_tiles, coarse_dest):
    scalars = pl.BlockSpec(memory_space=pltpu.SMEM)
    vmem = pl.BlockSpec(memory_space=pltpu.VMEM)
    hbm = pl.BlockSpec(memory_space=pltpu.HBM)
    anywhere = pl.BlockSpec(memory_space=pl.ANY)
    params = pltpu.CompilerParams(vmem_limit_bytes=24 * 2**20)
    prolong = prolong_tiles[0]
    numbers = jnp.concatenate(
        [
            panel_place(stiff_cols[0, 0]),
            stiff_rows[0, 0],
            product_slot[0, 0].reshape(KA * KP),
            coarse_dest.reshape(KP * KAP) % COARSE,
        ]
    )
    pieces, numbers = gather_pieces(prolong, numbers)
    sent = pl.pallas_call(
        product_kernel,
        out_shape=jax.ShapeDtypeStruct((COLS, BLOCK, TILE), jnp.bfloat16),
        in_specs=[scalars, hbm] + [anywhere] * len(PIECES),
        out_specs=hbm,
        scratch_shapes=[
            pltpu.VMEM((ROWS, TILE, SHARD), jnp.bfloat16),
            pltpu.VMEM((KA, TILE, TILE), jnp.bfloat16),
            pltpu.VMEM((COLS, BLOCK, TILE), jnp.bfloat16),
            pltpu.SMEM((KA,), jnp.int32),
            pltpu.SMEM((COLS,), jnp.int32),
            pltpu.SemaphoreType.DMA((len(PIECES) * KP,)),
            pltpu.SemaphoreType.DMA((1,)),
            pltpu.SemaphoreType.DMA((COLS,)),
        ],
        compiler_params=pltpu.CompilerParams(vmem_limit_bytes=K1_MIB * 2**20),
    )(numbers, stiff_tiles[0, 0], *pieces)
    got = lax.all_to_all(sent, "col", split_axis=0, concat_axis=0, tiled=True)
    chunk_total = 4
    ap, merged = pl.pallas_call(
        coarse_kernel,
        out_shape=(
            jax.ShapeDtypeStruct((KAP, TILE, TILE), jnp.bfloat16),
            jax.ShapeDtypeStruct((COARSE, TILE, TILE), jnp.bfloat16),
        ),
        in_specs=[scalars, vmem, hbm],
        out_specs=(vmem, hbm),
        scratch_shapes=[
            pltpu.VMEM((chunk_total, COLS // chunk_total, BODY, TILE), jnp.bfloat16),
            pltpu.VMEM((COLS, MARK, TILE), jnp.bfloat16),
            pltpu.VMEM((COLS, TILE), jnp.int32),
            pltpu.SMEM((COLS, TILE), jnp.int32),
            pltpu.VMEM((KAP, TILE, TILE), jnp.float32),
            pltpu.VMEM((COARSE, TILE, TILE), jnp.float32),
            pltpu.VMEM((COARSE, TILE, TILE), jnp.bfloat16),
            pltpu.SemaphoreType.DMA((chunk_total,)),
            pltpu.SemaphoreType.DMA((3,)),
        ],
        compiler_params=params,
    )(numbers, prolong, got)
    received = lax.all_to_all(merged, "col", split_axis=0, concat_axis=0, tiled=True)
    coarse = jnp.sum(received.reshape(COLS, CTD, TILE, TILE).astype(jnp.float32), axis=0)
    return (ap[None], coarse)


def solution(mesh):
    in_specs = (
        P("row", "col", None, None, None),
        P("row", "col", None),
        P("row", "col", None),
        P("row", "col", None, None),
        P(("row", "col"), None, None, None),
        P(("row", "col"), None, None),
    )
    out_specs = (P(("row", "col"), None, None, None), P(("row", "col"), None, None))
    return jax.shard_map(
        on_device, mesh=mesh, in_specs=in_specs, out_specs=out_specs, check_vma=False
    )
```

time: 162 us -> 143 us (0.88)
  the two profiles are of different devices: /device:TPU:96 before, /device:TPU:8 now
where the time goes in v2:
time: 143 us
  blocking collectives  106 us (74%)
  starting transfers between devices  12.1 us (8%)
  waiting for transfers between devices  9.92 us (7%)
  Pallas kernels  8.75 us (6%)
  other arithmetic  3.49 us (2%)
  local copies, waits for them, and re-layouts  1.99 us (1%)
    all_to_all x1, blocking collectives, on_device(): got = lax.all_to_all(sent, 'col', split_axis=0, concat_axis=0, tiled=True)  47 us
    all_gather x1, blocking collectives, gather_pieces(): lax.all_gather(prolong.reshape(SHARD, TILE), 'row', axis=0, tiled=True, a...  38.8 us
    all_to_all x1, blocking collectives, on_device(): lax.all_to_all(merged, 'col', split_axis=0, concat_axis=0, tiled=True)  19.7 us
    ppermute x2, waiting for transfers between devices, shifted(): return lax.ppermute(array, 'row', pairs)  8.61 us
    ppermute x3, starting transfers between devices, to_sibling(): return lax.ppermute(array, 'row', [(r, r ^ 1) for r in range(ROWS)])  6.23 us
    ppermute x2, starting transfers between devices, shifted(): return lax.ppermute(array, 'row', pairs)  5.84 us
    pallas_call x1, Pallas kernels, on_device(): pl.pallas_call(product_kernel, out_shape=jax.ShapeDtypeStruct((COLS, BLOC...  5 us
    pallas_call x1, Pallas kernels, on_device(): pl.pallas_call(coarse_kernel, out_shape=(jax.ShapeDtypeStruct((KAP, TILE,...  3.75 us
  transfers between devices with their start and end apart: 5, of which 3 were waited for; matrix products, arithmetic and copies ran while one was open for 3% of the time, Pallas kernels for 0%

profile of v2, /device:TPU:8, one launch (start us, length us, event | category | flops | bytes accessed | tf_op | source)
XLA Modules:
  0.0 142.5 jit_solution(8142044697508901119)
XLA Ops:
  0.6 38.8 %all_gather.3 = bf16[3072,128]{1,0:T(8,128)(2,1)S(1)} all-gather(bf16[384,128]{1,0:T(8,128)(2,1)} %bitcast.28), channel_id=1, replica_groups={{0,64,128,192,256,320,384,448},{16,80,144,208,272,336,400,464},{32,96,1..., dimensions={0}, use_global_device_ids=true | all-gather | bytes 884736 | tf_op jit(solution)/shard_map/all_gather | solution.py:135
  39.4 1.9 %collective-permute-start.2 = (bf16[3072,128]{1,0:T(8,128)(2,1)S(1)}, bf16[3072,128]{1,0:T(8,128)(2,1)S(1)}, u32[]{:S(2)}, u32[]{:S(2)}) collective-permute-start(bf16[3072,128]{1,0:T(8,128)(2,1)S(1)} %all_gather.3), channel_id=1, source_target_pairs={{0,16},{16,0},{32,48},{48,32},{64,80},{80,64},{96,112},{112,96},{1... | collective-permute-start | bytes 2359304 | tf_op jit(solution)/shard_map/ppermute | solution.py:130
  41.3 0.1 fusion.5
  41.4 3.8 %collective-permute-start.1 = (bf16[1536,128]{1,0:T(8,128)(2,1)S(1)}, bf16[1536,128]{1,0:T(8,128)(2,1)S(1)}, u32[]{:S(2)}, u32[]{:S(2)}) collective-permute-start(bf16[1536,128]{1,0:T(8,128)(2,1)S(1)} %get-tuple-element.12), channel_id=1, source_target_pairs={{0,480},{16,496},{32,0},{48,16},{64,32},{80,48},{96,64},{112,80},{... | collective-permute-start | bytes 1179656 | tf_op jit(solution)/shard_map/ppermute | solution.py:126
  45.2 2.1 %collective-permute-start = (bf16[1536,128]{1,0:T(8,128)(2,1)S(1)}, bf16[1536,128]{1,0:T(8,128)(2,1)S(1)}, u32[]{:S(2)}, u32[]{:S(2)}) collective-permute-start(bf16[1536,128]{1,0:T(8,128)(2,1)S(1)} %get-tuple-element.13), channel_id=1, source_target_pairs={{0,32},{16,48},{32,64},{48,80},{64,96},{80,112},{96,128},{112,144}... | collective-permute-start | bytes 1179656 | tf_op jit(solution)/shard_map/ppermute | solution.py:126
  47.3 0.7 reduce
  48.0 0.1 reshape.28
  48.1 0.8 copy.9
  48.8 0.1 reshape_squeeze.7
  48.9 0.7 fusion.1
  49.6 1.3 pad_add_fusion.scalar_ref
  50.9 3.9 %collective-permute-done.1 = bf16[1536,128]{1,0:T(8,128)(2,1)S(1)} collective-permute-done((bf16[1536,128]{1,0:T(8,128)(2,1)S(1)}, bf16[1536,128]{1,0:T(8,128)(2,1)S(1)}, u32[]{:S(2)}, u32[]{:S(2)}) %collective-permute-start.1) | collective-permute-done | bytes 393248 | tf_op jit(solution)/shard_map/ppermute | solution.py:126
  54.8 4.7 %collective-permute-done = bf16[1536,128]{1,0:T(8,128)(2,1)S(1)} collective-permute-done((bf16[1536,128]{1,0:T(8,128)(2,1)S(1)}, bf16[1536,128]{1,0:T(8,128)(2,1)S(1)}, u32[]{:S(2)}, u32[]{:S(2)}) %collective-permute-start) | collective-permute-done | bytes 393248 | tf_op jit(solution)/shard_map/ppermute | solution.py:126
  59.5 1.9 %collective-permute-start.3 = (bf16[1536,128]{1,0:T(8,128)(2,1)S(1)}, bf16[1536,128]{1,0:T(8,128)(2,1)S(1)}, u32[]{:S(2)}, u32[]{:S(2)}) collective-permute-start(bf16[1536,128]{1,0:T(8,128)(2,1)S(1)} %collective-permute-done), channel_id=1, source_target_pairs={{0,16},{16,0},{32,48},{48,32},{64,80},{80,64},{96,112},{112,96},{1... | collective-permute-start | bytes 1179656 | tf_op jit(solution)/shard_map/ppermute | solution.py:130
  61.4 2.4 %collective-permute-start.4 = (bf16[1536,128]{1,0:T(8,128)(2,1)S(1)}, bf16[1536,128]{1,0:T(8,128)(2,1)S(1)}, u32[]{:S(2)}, u32[]{:S(2)}) collective-permute-start(bf16[1536,128]{1,0:T(8,128)(2,1)S(1)} %collective-permute-done.1), channel_id=1, source_target_pairs={{0,16},{16,0},{32,48},{48,32},{64,80},{80,64},{96,112},{112,96},{1... | collective-permute-start | bytes 1179656 | tf_op jit(solution)/shard_map/ppermute | solution.py:130
  63.9 1.3 collective-permute-done.4
  65.2 0.7 copy-done.7
  65.9 0.3 copy-done.3
  66.2 5.0 %shard_map.77 = bf16[16,784,128]{2,1,0:T(8,128)(2,1)} custom-call(s32[184]{0:T(256)} %pad_add_fusion.scalar_ref, bf16[32,128,128]{2,1,0:T(8,128)(2,1)} %bitcast.32, bf16[8,3,128,128]{3,2,1,0:T(8,128)(2,1)} %bitcast.30, bf16[4,3,128,128]{3,2,1,0:T(8,128)(2,1)} %bitcast.35, bf16[4,3,128,128]{3,2,1,0:T(8,128)(2,1)} %bitcast.34, ...), custom_call_target="tpu_custom_call" | custom-call | tf_op jit(solution)/shard_map/pallas_call | solution.py:172
  71.2 0.0 copy-start
  71.2 47.0 %all_to_all.10.got_ref = bf16[16,784,128]{2,1,0:T(8,128)(2,1)S(1)} all-to-all(bf16[16,784,128]{2,1,0:T(8,128)(2,1)} %shard_map.77), channel_id=1, replica_groups=mesh['row'=32,'col'=16] {'col'}, dimensions={0} | all-to-all | bytes 6422528 | tf_op jit(solution)/shard_map/all_to_all | solution.py:189
  118.2 3.7 %shard_map.78 = (bf16[8,128,128]{2,1,0:T(8,128)(2,1)}, bf16[32,128,128]{2,1,0:T(8,128)(2,1)S(1)}) custom-call(s32[184]{0:T(256)S(1)} %copy-done.1, bf16[3,128,128]{2,1,0:T(8,128)(2,1)S(1)} %bitcast.29, bf16[16,784,128]{2,1,0:T(8,128)(2,1)S(1)} %all_to_all.10.got_ref), custom_call_target="tpu_custom_call" | custom-call | tf_op jit(solution)/shard_map/pallas_call | solution.py:191
  122.0 19.7 %all_to_all.11 = bf16[32,128,128]{2,1,0:T(8,128)(2,1)S(1)} all-to-all(bf16[32,128,128]{2,1,0:T(8,128)(2,1)S(1)} %get-tuple-element.11), channel_id=1, replica_groups=mesh['row'=32,'col'=16] {'col'}, dimensions={0} | all-to-all | bytes 2097152 | tf_op jit(solution)/shard_map/all_to_all | solution.py:212
  141.7 0.8 convert_reduce_fusion
  (16 shorter events, 0.0 us)
Async XLA Ops:
  39.4 25.8 %copy-start.2 = (bf16[3072,128]{1,0:T(8,128)(2,1)}, bf16[3072,128]{1,0:T(8,128)(2,1)S(1)}, u32[]{:S(2)}) copy-start(bf16[3072,128]{1,0:T(8,128)(2,1)S(1)} %all_gather.3) | copy-start | bytes 2359300
  39.4 25.8 %collective-permute-start.2 = (bf16[3072,128]{1,0:T(8,128)(2,1)S(1)}, bf16[3072,128]{1,0:T(8,128)(2,1)S(1)}, u32[]{:S(2)}, u32[]{:S(2)}) collective-permute-start(bf16[3072,128]{1,0:T(8,128)(2,1)S(1)} %all_gather.3), channel_id=1, source_target_pairs={{0,16},{16,0},{32,48},{48,32},{64,80},{80,64},{96,112},{112,96},{1... | collective-permute-start | bytes 2359304 | tf_op jit(solution)/shard_map/ppermute | solution.py:130
  41.4 13.4 %collective-permute-start.1 = (bf16[1536,128]{1,0:T(8,128)(2,1)S(1)}, bf16[1536,128]{1,0:T(8,128)(2,1)S(1)}, u32[]{:S(2)}, u32[]{:S(2)}) collective-permute-start(bf16[1536,128]{1,0:T(8,128)(2,1)S(1)} %get-tuple-element.12), channel_id=1, source_target_pairs={{0,480},{16,496},{32,0},{48,16},{64,32},{80,48},{96,64},{112,80},{... | collective-permute-start | bytes 1179656 | tf_op jit(solution)/shard_map/ppermute | solution.py:126
  45.2 14.3 %collective-permute-start = (bf16[1536,128]{1,0:T(8,128)(2,1)S(1)}, bf16[1536,128]{1,0:T(8,128)(2,1)S(1)}, u32[]{:S(2)}, u32[]{:S(2)}) collective-permute-start(bf16[1536,128]{1,0:T(8,128)(2,1)S(1)} %get-tuple-element.13), channel_id=1, source_target_pairs={{0,32},{16,48},{32,64},{48,80},{64,96},{80,112},{96,128},{112,144}... | collective-permute-start | bytes 1179656 | tf_op jit(solution)/shard_map/ppermute | solution.py:126
  54.8 10.4 %copy-start.4 = (bf16[1536,128]{1,0:T(8,128)(2,1)}, bf16[1536,128]{1,0:T(8,128)(2,1)S(1)}, u32[]{:S(2)}) copy-start(bf16[1536,128]{1,0:T(8,128)(2,1)S(1)} %collective-permute-done.1) | copy-start | bytes 1179652
  59.5 5.7 %copy-start.5 = (bf16[1536,128]{1,0:T(8,128)(2,1)}, bf16[1536,128]{1,0:T(8,128)(2,1)S(1)}, u32[]{:S(2)}) copy-start(bf16[1536,128]{1,0:T(8,128)(2,1)S(1)} %collective-permute-done) | copy-start | bytes 1179652
  59.5 4.3 %collective-permute-start.3 = (bf16[1536,128]{1,0:T(8,128)(2,1)S(1)}, bf16[1536,128]{1,0:T(8,128)(2,1)S(1)}, u32[]{:S(2)}, u32[]{:S(2)}) collective-permute-start(bf16[1536,128]{1,0:T(8,128)(2,1)S(1)} %collective-permute-done), channel_id=1, source_target_pairs={{0,16},{16,0},{32,48},{48,32},{64,80},{80,64},{96,112},{112,96},{1... | collective-permute-start | bytes 1179656 | tf_op jit(solution)/shard_map/ppermute | solution.py:130
  61.4 3.7 %collective-permute-start.4 = (bf16[1536,128]{1,0:T(8,128)(2,1)S(1)}, bf16[1536,128]{1,0:T(8,128)(2,1)S(1)}, u32[]{:S(2)}, u32[]{:S(2)}) collective-permute-start(bf16[1536,128]{1,0:T(8,128)(2,1)S(1)} %collective-permute-done.1), channel_id=1, source_target_pairs={{0,16},{16,0},{32,48},{48,32},{64,80},{80,64},{96,112},{112,96},{1... | collective-permute-start | bytes 1179656 | tf_op jit(solution)/shard_map/ppermute | solution.py:130
  63.9 1.4 copy-start.6
  65.2 0.7 copy-start.7
  65.2 1.0 copy-start.3
  71.2 47.0 %copy-start = (bf16[1,3,128,128]{3,2,1,0:T(8,128)(2,1)S(1)}, bf16[1,3,128,128]{3,2,1,0:T(8,128)(2,1)}, u32[]{:S(2)}) copy-start(bf16[1,3,128,128]{3,2,1,0:T(8,128)(2,1)} %param.10) | copy-start | bytes 294916
  71.2 47.0 %copy-start.1 = (s32[184]{0:T(256)S(1)}, s32[184]{0:T(256)}, u32[]{:S(2)}) copy-start(s32[184]{0:T(256)} %pad_add_fusion.scalar_ref) | copy-start | bytes 2212

commit v3 on v2

--- a/solution.py
+++ b/solution.py
@@ -19,13 +19,13 @@
 MARK = 16
 BLOCK = BODY + MARK
 COARSE = COLS * CTD
-K1_MIB = 57
+K1_MIB = 24
 SPOT = 2 * KA + KA * KP
 
 
 def product_kernel(scalar_ref, tile_ref, *rest):
     pieces = rest[: len(PIECES)]
-    out_ref, panel, tiles, outs, order, count, sems, tile_sem, out_sems = rest[len(PIECES) :]
+    outs, panel, tiles, order, count, sems, tile_sem = rest[len(PIECES) :]
     tile_copy = pltpu.make_async_copy(tile_ref, tiles, tile_sem.at[0])
     tile_copy.start()
     copies = []
@@ -51,7 +51,6 @@
     tile_copy.wait()
     for copy in copies:
         copy.wait()
-    out_copies = []
     for owner in range(COLS):
         mark = jnp.zeros((MARK, TILE), jnp.float32)
         for which in range(PAIR):
@@ -65,11 +64,6 @@
                 value = scalar_ref[2 * KA + t * KP + k].astype(jnp.float32)
                 mark = jnp.where(lane == q, value, mark)
         outs[owner, BODY:, :] = mark.astype(jnp.bfloat16)
-        out_copy = pltpu.make_async_copy(outs.at[owner], out_ref.at[owner], out_sems.at[owner])
-        out_copy.start()
-        out_copies.append(out_copy)
-    for out_copy in out_copies:
-        out_copy.wait()
 
 
 def coarse_kernel(
@@ -116,12 +110,14 @@
     out_copy.wait()
 
 
-PIECES = ((0, 8), (8, 4), (12, 4), (16, 8), (24, 4), (28, 4))
-
-
-def shifted(array, step):
+PIECES = ((0, 16), (16, 16))
+
+
+def from_neighbour(array):
     pairs = [
-        (2 * z + core, 2 * ((z + step) % RINGS) + core) for z in range(RINGS) for core in range(2)
+        (2 * z + core, 2 * ((z + (1 if core == 0 else -1)) % RINGS) + core)
+        for z in range(RINGS)
+        for core in range(2)
     ]
     return lax.ppermute(array, "row", pairs)
 
@@ -132,14 +128,13 @@
 
 def gather_pieces(prolong, numbers):
     groups = [[2 * (low + 2 * k) + core for k in range(8)] for low in range(2) for core in range(2)]
-    own8 = lax.all_gather(
+    same8 = lax.all_gather(
         prolong.reshape(SHARD, TILE), "row", axis=0, tiled=True, axis_index_groups=groups
     )
-    other8 = to_sibling(own8)
-    low4 = shifted(own8[: 4 * SHARD], 1)
-    high4 = shifted(own8[4 * SHARD :], -1)
-    low4, high4, numbers = lax.optimization_barrier((low4, high4, numbers))
-    pieces = [own8, low4, high4, other8, to_sibling(low4), to_sibling(high4)]
+    next8 = from_neighbour(same8)
+    next8, numbers = lax.optimization_barrier((next8, numbers))
+    own16 = jnp.concatenate([same8, next8])
+    pieces = [own16, to_sibling(own16)]
     return [piece.reshape(-1, KP, TILE, TILE) for piece in pieces], numbers
 
 
@@ -173,16 +168,14 @@
         product_kernel,
         out_shape=jax.ShapeDtypeStruct((COLS, BLOCK, TILE), jnp.bfloat16),
         in_specs=[scalars, hbm] + [anywhere] * len(PIECES),
-        out_specs=hbm,
+        out_specs=vmem,
         scratch_shapes=[
             pltpu.VMEM((ROWS, TILE, SHARD), jnp.bfloat16),
             pltpu.VMEM((KA, TILE, TILE), jnp.bfloat16),
-            pltpu.VMEM((COLS, BLOCK, TILE), jnp.bfloat16),
             pltpu.SMEM((KA,), jnp.int32),
             pltpu.SMEM((COLS,), jnp.int32),
             pltpu.SemaphoreType.DMA((len(PIECES) * KP,)),
             pltpu.SemaphoreType.DMA((1,)),
-            pltpu.SemaphoreType.DMA((COLS,)),
         ],
         compiler_params=pltpu.CompilerParams(vmem_limit_bytes=K1_MIB * 2**20),
     )(numbers, stiff_tiles[0, 0], *pieces)

time: 143 us -> 133 us (0.930)
  starting transfers between devices: 12.1 us -> 5.61 us
  Pallas kernels: 8.75 us -> 6.14 us
  waiting for transfers between devices: 9.92 us -> 11.6 us
    ppermute x3 -> x1, starting transfers between devices: 6.23 us -> 1.92 us  [to_sibling(): return lax.ppermute(array, 'row', [(r, r ^ 1) for r in range(ROWS)])]
    pallas_call x1, Pallas kernels: 5 us -> 2.38 us  [on_device(): pl.pallas_call(product_kernel, out_shape=jax.ShapeDtypeStruct((COLS, BLOC...]
    ppermute x2 -> x1, starting transfers between devices: 5.84 us -> 3.69 us  [from_neighbour(): return lax.ppermute(array, 'row', pairs)]
    ppermute x3 -> x1, waiting for transfers between devices: 1.31 us -> 3.38 us  [to_sibling(): return lax.ppermute(array, 'row', [(r, r ^ 1) for r in range(ROWS)])]
    ppermute x2 -> x1, waiting for transfers between devices: 8.61 us -> 8.24 us  [from_neighbour(): return lax.ppermute(array, 'row', pairs)]
  transfers between devices with their start and end apart: 5 -> 2, of which waited for: 3 -> 2; matrix products, arithmetic and copies ran while one was open for 3% -> 2% of each run, Pallas kernels for 0% -> 0%
where the time goes in v3:
time: 133 us
  blocking collectives  105 us (79%)
  waiting for transfers between devices  11.6 us (9%)
  Pallas kernels  6.14 us (5%)
  starting transfers between devices  5.61 us (4%)
  other arithmetic  2.93 us (2%)
    all_to_all x1, blocking collectives, on_device(): got = lax.all_to_all(sent, 'col', split_axis=0, concat_axis=0, tiled=True)  46.6 us
    all_gather x1, blocking collectives, gather_pieces(): lax.all_gather(prolong.reshape(SHARD, TILE), 'row', axis=0, tiled=True, a...  38.8 us
    all_to_all x1, blocking collectives, on_device(): lax.all_to_all(merged, 'col', split_axis=0, concat_axis=0, tiled=True)  19.5 us
    ppermute x1, waiting for transfers between devices, from_neighbour(): return lax.ppermute(array, 'row', pairs)  8.24 us
    pallas_call x1, Pallas kernels, on_device(): pl.pallas_call(coarse_kernel, out_shape=(jax.ShapeDtypeStruct((KAP, TILE,...  3.76 us
    ppermute x1, starting transfers between devices, from_neighbour(): return lax.ppermute(array, 'row', pairs)  3.69 us
    ppermute x1, waiting for transfers between devices, to_sibling(): return lax.ppermute(array, 'row', [(r, r ^ 1) for r in range(ROWS)])  3.38 us
  transfers between devices with their start and end apart: 2, of which 2 were waited for; matrix products, arithmetic and copies ran while one was open for 2% of the time, Pallas kernels for 0%

profile of v3, /device:TPU:8, one launch (start us, length us, event | category | flops | bytes accessed | tf_op | source)
XLA Modules:
  0.0 132.9 jit_solution(18429113890712836886)
XLA Ops:
  0.6 38.8 %all_gather.3 = bf16[3072,128]{1,0:T(8,128)(2,1)S(1)} all-gather(bf16[384,128]{1,0:T(8,128)(2,1)} %bitcast.27), channel_id=1, replica_groups={{0,64,128,192,256,320,384,448},{16,80,144,208,272,336,400,464},{32,96,1..., dimensions={0}, use_global_device_ids=true | all-gather | bytes 884736 | tf_op jit(solution)/shard_map/all_gather | solution.py:131
  39.4 3.7 %collective-permute-start = (bf16[3072,128]{1,0:T(8,128)(2,1)S(1)}, bf16[3072,128]{1,0:T(8,128)(2,1)S(1)}, u32[]{:S(2)}, u32[]{:S(2)}) collective-permute-start(bf16[3072,128]{1,0:T(8,128)(2,1)S(1)} %all_gather.3), channel_id=1, source_target_pairs={{0,32},{16,496},{32,64},{48,16},{64,96},{80,48},{96,128},{112,80},... | collective-permute-start | bytes 2359304 | tf_op jit(solution)/shard_map/ppermute | solution.py:122
  43.1 0.7 reduce
  43.8 0.1 reshape.16
  43.9 0.8 copy.9
  44.7 0.1 reshape_squeeze.7
  44.8 0.7 fusion.1
  45.5 0.7 pad_add_fusion.scalar_ref
  46.2 0.0 copy-start
  46.2 0.1 constant_dynamic-update-slice_fusion.1
  46.3 8.2 %collective-permute-done = bf16[3072,128]{1,0:T(8,128)(2,1)S(1)} collective-permute-done((bf16[3072,128]{1,0:T(8,128)(2,1)S(1)}, bf16[3072,128]{1,0:T(8,128)(2,1)S(1)}, u32[]{:S(2)}, u32[]{:S(2)}) %collective-permute-start) | collective-permute-done | bytes 786464 | tf_op jit(solution)/shard_map/ppermute | solution.py:122
  54.5 0.1 constant_dynamic-update-slice_fusion
  54.6 1.9 %collective-permute-start.1 = (bf16[6144,128]{1,0:T(8,128)(2,1)S(1)}, bf16[6144,128]{1,0:T(8,128)(2,1)S(1)}, u32[]{:S(2)}, u32[]{:S(2)}) collective-permute-start(bf16[6144,128]{1,0:T(8,128)(2,1)S(1)} %constant_dynamic-update-slice_fusion), channel_id=1, source_target_pairs={{0,16},{16,0},{32,48},{48,32},{64,80},{80,64},{96,112},{112,96},{1... | collective-permute-start | bytes 4718600 | tf_op jit(solution)/shard_map/ppermute | solution.py:126
  56.5 3.4 %collective-permute-done.1 = bf16[6144,128]{1,0:T(8,128)(2,1)S(1)} collective-permute-done((bf16[6144,128]{1,0:T(8,128)(2,1)S(1)}, bf16[6144,128]{1,0:T(8,128)(2,1)S(1)}, u32[]{:S(2)}, u32[]{:S(2)}) %collective-permute-start.1) | collective-permute-done | bytes 1572896 | tf_op jit(solution)/shard_map/ppermute | solution.py:126
  59.9 0.0 copy-done
  59.9 2.4 %shard_map.77 = bf16[16,784,128]{2,1,0:T(8,128)(2,1)S(1)} custom-call(s32[184]{0:T(256)S(1)} %pad_add_fusion.scalar_ref, bf16[32,128,128]{2,1,0:T(8,128)(2,1)S(1)} %bitcast.26, bf16[16,3,128,128]{3,2,1,0:T(8,128)(2,1)S(1)} %bitcast.24, bf16[16,3,128,128]{3,2,1,0:T(8,128)(2,1)S(1)} %bitcast.25), custom_call_target="tpu_custom_call" | custom-call | tf_op jit(solution)/shard_map/pallas_call | solution.py:167
  62.3 0.0 copy-start.1
  62.3 46.6 %all_to_all.10.got_ref = bf16[16,784,128]{2,1,0:T(8,128)(2,1)S(1)} all-to-all(bf16[16,784,128]{2,1,0:T(8,128)(2,1)S(1)} %shard_map.77), channel_id=1, replica_groups=mesh['row'=32,'col'=16] {'col'}, dimensions={0} | all-to-all | bytes 6422528 | tf_op jit(solution)/shard_map/all_to_all | solution.py:182
  108.9 0.0 copy-done.1
  108.9 3.8 %shard_map.78 = (bf16[8,128,128]{2,1,0:T(8,128)(2,1)}, bf16[32,128,128]{2,1,0:T(8,128)(2,1)S(1)}) custom-call(s32[184]{0:T(256)S(1)} %pad_add_fusion.scalar_ref, bf16[3,128,128]{2,1,0:T(8,128)(2,1)S(1)} %bitcast.28, bf16[16,784,128]{2,1,0:T(8,128)(2,1)S(1)} %all_to_all.10.got_ref), custom_call_target="tpu_custom_call" | custom-call | tf_op jit(solution)/shard_map/pallas_call | solution.py:184
  112.7 19.5 %all_to_all.11 = bf16[32,128,128]{2,1,0:T(8,128)(2,1)S(1)} all-to-all(bf16[32,128,128]{2,1,0:T(8,128)(2,1)S(1)} %get-tuple-element.9), channel_id=1, replica_groups=mesh['row'=32,'col'=16] {'col'}, dimensions={0} | all-to-all | bytes 2097152 | tf_op jit(solution)/shard_map/all_to_all | solution.py:205
  132.1 0.8 convert_reduce_fusion
  (1 shorter events, 0.0 us)
Async XLA Ops:
  39.4 15.1 %collective-permute-start = (bf16[3072,128]{1,0:T(8,128)(2,1)S(1)}, bf16[3072,128]{1,0:T(8,128)(2,1)S(1)}, u32[]{:S(2)}, u32[]{:S(2)}) collective-permute-start(bf16[3072,128]{1,0:T(8,128)(2,1)S(1)} %all_gather.3), channel_id=1, source_target_pairs={{0,32},{16,496},{32,64},{48,16},{64,96},{80,48},{96,128},{112,80},... | collective-permute-start | bytes 2359304 | tf_op jit(solution)/shard_map/ppermute | solution.py:122
  46.2 13.7 %copy-start = (bf16[1,1,32,128,128]{4,3,2,1,0:T(8,128)(2,1)S(1)}, bf16[1,1,32,128,128]{4,3,2,1,0:T(8,128)(2,1)}, u32[]{:S(2)}) copy-start(bf16[1,1,32,128,128]{4,3,2,1,0:T(8,128)(2,1)} %param.6) | copy-start | bytes 3145732
  54.6 5.3 %collective-permute-start.1 = (bf16[6144,128]{1,0:T(8,128)(2,1)S(1)}, bf16[6144,128]{1,0:T(8,128)(2,1)S(1)}, u32[]{:S(2)}, u32[]{:S(2)}) collective-permute-start(bf16[6144,128]{1,0:T(8,128)(2,1)S(1)} %constant_dynamic-update-slice_fusion), channel_id=1, source_target_pairs={{0,16},{16,0},{32,48},{48,32},{64,80},{80,64},{96,112},{112,96},{1... | collective-permute-start | bytes 4718600 | tf_op jit(solution)/shard_map/ppermute | solution.py:126
  62.3 46.6 %copy-start.1 = (bf16[1,3,128,128]{3,2,1,0:T(8,128)(2,1)S(1)}, bf16[1,3,128,128]{3,2,1,0:T(8,128)(2,1)}, u32[]{:S(2)}) copy-start(bf16[1,3,128,128]{3,2,1,0:T(8,128)(2,1)} %param.10) | copy-start | bytes 294916

commit v4 on v3

--- a/solution.py
+++ b/solution.py
@@ -8,6 +8,7 @@
 TILE = 128
 KP = 3
 KAP = 8
+SIDE = 4
 CTD = 2
 COLS = 16
 RINGS = 16
@@ -51,7 +52,9 @@
     tile_copy.wait()
     for copy in copies:
         copy.wait()
-    for owner in range(COLS):
+    flipped = scalar_ref[SPOT + KP * KAP]
+    for place in range(COLS):
+        owner = jnp.where(flipped == 0, place, place % SIDE * SIDE + place // SIDE)
         mark = jnp.zeros((MARK, TILE), jnp.float32)
         for which in range(PAIR):
             t = order[owner * PAIR + which]
@@ -60,43 +63,36 @@
             ).astype(jnp.bfloat16)
             for k in range(KP):
                 q = which * KP + k
-                outs[owner, q * TILE : (q + 1) * TILE, :] = product[:, k * TILE : (k + 1) * TILE]
+                outs[place, q * TILE : (q + 1) * TILE, :] = product[:, k * TILE : (k + 1) * TILE]
                 value = scalar_ref[2 * KA + t * KP + k].astype(jnp.float32)
                 mark = jnp.where(lane == q, value, mark)
-        outs[owner, BODY:, :] = mark.astype(jnp.bfloat16)
-
-
-def coarse_kernel(
-    scalar_ref, prolong_ref, got_ref, ap_ref, out_ref,
-    held, mark_held, mark_int, mark_scalar, total, merged, rounded, sems, mark_sems,
-):
-    chunk_total = held.shape[0]
-    chunk = COLS // chunk_total
-    mark_copy = pltpu.make_async_copy(got_ref.at[:, pl.ds(BODY, MARK), :], mark_held, mark_sems.at[0])
-    mark_copy.start()
-    copies = [
-        pltpu.make_async_copy(
-            got_ref.at[pl.ds(index * chunk, chunk), pl.ds(0, BODY), :], held.at[index], sems.at[index]
-        )
-        for index in range(chunk_total)
-    ]
-    for copy in copies:
-        copy.start()
-    mark_copy.wait()
-    mark_int[...] = mark_held[...].astype(jnp.float32)[:, 0, :].astype(jnp.int32)
-    scalar_copy = pltpu.make_async_copy(mark_int, mark_scalar, mark_sems.at[1])
+        outs[place, BODY:, :] = mark.astype(jnp.bfloat16)
+
+
+def slot_kernel(got_ref, out_ref, mark_int, mark_scalar, total, sem):
+    marks = got_ref[:, BODY:, :].astype(jnp.float32)
+    mark_int[...] = marks[:, 0, :].astype(jnp.int32)
+    scalar_copy = pltpu.make_async_copy(mark_int, mark_scalar, sem.at[0])
     scalar_copy.start()
     total[...] = jnp.zeros_like(total)
+    scalar_copy.wait()
+    for peer in range(SIDE):
+        for owner in range(SIDE):
+            block = peer * SIDE + owner
+            for q in range(PAIR * KP):
+                where = owner * KAP + mark_scalar[block, q]
+                part = got_ref[block, q * TILE : (q + 1) * TILE, :]
+                total[where] = total[where] + part.astype(jnp.float32)
+    out_ref[...] = total[...].astype(jnp.bfloat16)
+
+
+def coarse_kernel(scalar_ref, prolong_ref, got_ref, ap_ref, out_ref, merged):
     merged[...] = jnp.zeros_like(merged)
-    scalar_copy.wait()
-    for index in range(chunk_total):
-        copies[index].wait()
-        for peer in range(chunk):
-            for q in range(PAIR * KP):
-                slot = mark_scalar[index * chunk + peer, q]
-                total[slot] = total[slot] + held[index, peer, pl.ds(q * TILE, TILE), :].astype(jnp.float32)
     for s in range(KAP):
-        ap = total[s].astype(jnp.bfloat16)
+        total = got_ref[s].astype(jnp.float32)
+        for peer in range(1, SIDE):
+            total = total + got_ref[peer * KAP + s].astype(jnp.float32)
+        ap = total.astype(jnp.bfloat16)
         ap_ref[s] = ap
         for k in range(KP):
             term = lax.dot_general(
@@ -104,10 +100,32 @@
             )
             bucket = scalar_ref[SPOT + k * KAP + s]
             merged[bucket] = merged[bucket] + term
-    rounded[...] = merged[...].astype(jnp.bfloat16)
-    out_copy = pltpu.make_async_copy(rounded, out_ref, mark_sems.at[2])
-    out_copy.start()
-    out_copy.wait()
+    out_ref[...] = merged[...].astype(jnp.bfloat16)
+
+
+def side_groups(even_along_x):
+    groups = []
+    for row in range(ROWS):
+        along_x = (row % 2 == 0) == even_along_x
+        for fixed in range(SIDE):
+            groups.append(
+                [
+                    row * COLS + (move * SIDE + fixed if along_x else fixed * SIDE + move)
+                    for move in range(SIDE)
+                ]
+            )
+    return groups
+
+
+def exchange_side(array, even_along_x):
+    return lax.all_to_all(
+        array,
+        ("row", "col"),
+        split_axis=0,
+        concat_axis=0,
+        tiled=True,
+        axis_index_groups=side_groups(even_along_x),
+    )
 
 
 PIECES = ((0, 16), (16, 16))
@@ -161,6 +179,7 @@
             stiff_rows[0, 0],
             product_slot[0, 0].reshape(KA * KP),
             coarse_dest.reshape(KP * KAP) % COARSE,
+            jnp.full((1,), lax.axis_index("row") % 2, jnp.int32),
         ]
     )
     pieces, numbers = gather_pieces(prolong, numbers)
@@ -179,29 +198,32 @@
         ],
         compiler_params=pltpu.CompilerParams(vmem_limit_bytes=K1_MIB * 2**20),
     )(numbers, stiff_tiles[0, 0], *pieces)
-    got = lax.all_to_all(sent, "col", split_axis=0, concat_axis=0, tiled=True)
-    chunk_total = 4
+    got = exchange_side(sent, True)
+    partial = pl.pallas_call(
+        slot_kernel,
+        out_shape=jax.ShapeDtypeStruct((SIDE * KAP, TILE, TILE), jnp.bfloat16),
+        in_specs=[vmem],
+        out_specs=vmem,
+        scratch_shapes=[
+            pltpu.VMEM((COLS, TILE), jnp.int32),
+            pltpu.SMEM((COLS, TILE), jnp.int32),
+            pltpu.VMEM((SIDE * KAP, TILE, TILE), jnp.float32),
+            pltpu.SemaphoreType.DMA((1,)),
+        ],
+        compiler_params=params,
+    )(got)
+    summed = exchange_side(partial, False)
     ap, merged = pl.pallas_call(
         coarse_kernel,
         out_shape=(
             jax.ShapeDtypeStruct((KAP, TILE, TILE), jnp.bfloat16),
             jax.ShapeDtypeStruct((COARSE, TILE, TILE), jnp.bfloat16),
         ),
-        in_specs=[scalars, vmem, hbm],
-        out_specs=(vmem, hbm),
-        scratch_shapes=[
-            pltpu.VMEM((chunk_total, COLS // chunk_total, BODY, TILE), jnp.bfloat16),
-            pltpu.VMEM((COLS, MARK, TILE), jnp.bfloat16),
-            pltpu.VMEM((COLS, TILE), jnp.int32),
-            pltpu.SMEM((COLS, TILE), jnp.int32),
-            pltpu.VMEM((KAP, TILE, TILE), jnp.float32),
-            pltpu.VMEM((COARSE, TILE, TILE), jnp.float32),
-            pltpu.VMEM((COARSE, TILE, TILE), jnp.bfloat16),
-            pltpu.SemaphoreType.DMA((chunk_total,)),
-            pltpu.SemaphoreType.DMA((3,)),
-        ],
+        in_specs=[scalars, vmem, vmem],
+        out_specs=(vmem, vmem),
+        scratch_shapes=[pltpu.VMEM((COARSE, TILE, TILE), jnp.float32)],
         compiler_params=params,
-    )(numbers, prolong, got)
+    )(numbers, prolong, summed)
     received = lax.all_to_all(merged, "col", split_axis=0, concat_axis=0, tiled=True)
     coarse = jnp.sum(received.reshape(COLS, CTD, TILE, TILE).astype(jnp.float32), axis=0)
     return (ap[None], coarse)

time: 133 us -> 126 us (0.947)
  blocking collectives: 105 us -> 97.3 us
    all_to_all x1 -> x2, blocking collectives: 46.6 us -> 40.9 us  [exchange_side(): lax.all_to_all(array, ('row', 'col'), split_axis=0, concat_axis=0, tiled=...]
    pallas_call x1, Pallas kernels: 3.76 us -> 1.73 us  [on_device(): pl.pallas_call(coarse_kernel, out_shape=(jax.ShapeDtypeStruct((KAP, TILE,...]
    all_to_all x1, blocking collectives: 19.5 us -> 17.6 us  [on_device(): lax.all_to_all(merged, 'col', split_axis=0, concat_axis=0, tiled=True)]
    pallas_call x0 -> x1, Pallas kernels: none -> 1.83 us  [on_device(): pl.pallas_call(slot_kernel, out_shape=jax.ShapeDtypeStruct((SIDE * KAP, T...]
where the time goes in v4:
time: 126 us; the launch traced here: 125 us
  blocking collectives  97.3 us (77%)
  waiting for transfers between devices  11.6 us (9%)
  Pallas kernels  5.94 us (5%)
  starting transfers between devices  5.61 us (4%)
  other arithmetic  2.19 us (2%)
  local copies, waits for them, and re-layouts  1.85 us (1%)
    all_to_all x2, blocking collectives, exchange_side(): lax.all_to_all(array, ('row', 'col'), split_axis=0, concat_axis=0, tiled=...  40.9 us
    all_gather x1, blocking collectives, gather_pieces(): lax.all_gather(prolong.reshape(SHARD, TILE), 'row', axis=0, tiled=True, a...  38.8 us
    all_to_all x1, blocking collectives, on_device(): lax.all_to_all(merged, 'col', split_axis=0, concat_axis=0, tiled=True)  17.6 us
    ppermute x1, waiting for transfers between devices, from_neighbour(): return lax.ppermute(array, 'row', pairs)  8.21 us
    ppermute x1, starting transfers between devices, from_neighbour(): return lax.ppermute(array, 'row', pairs)  3.69 us
    ppermute x1, waiting for transfers between devices, to_sibling(): return lax.ppermute(array, 'row', [(r, r ^ 1) for r in range(ROWS)])  3.38 us
  transfers between devices with their start and end apart: 2, of which 2 were waited for; matrix products, arithmetic and copies ran while one was open for 2% of the time, Pallas kernels for 0%

profile of v4, /device:TPU:8, one launch (start us, length us, event | category | flops | bytes accessed | tf_op | source)
XLA Modules:
  0.0 125.2 jit_solution(13015152313461885918)
XLA Ops:
  0.6 38.8 %all_gather.3 = bf16[3072,128]{1,0:T(8,128)(2,1)S(1)} all-gather(bf16[384,128]{1,0:T(8,128)(2,1)} %bitcast.28), channel_id=1, replica_groups={{0,64,128,192,256,320,384,448},{16,80,144,208,272,336,400,464},{32,96,1..., dimensions={0}, use_global_device_ids=true | all-gather | bytes 884736 | tf_op jit(solution)/shard_map/all_gather | solution.py:149
  39.4 3.7 %collective-permute-start = (bf16[3072,128]{1,0:T(8,128)(2,1)S(1)}, bf16[3072,128]{1,0:T(8,128)(2,1)S(1)}, u32[]{:S(2)}, u32[]{:S(2)}) collective-permute-start(bf16[3072,128]{1,0:T(8,128)(2,1)S(1)} %all_gather.3), channel_id=1, source_target_pairs={{0,32},{16,496},{32,64},{48,16},{64,96},{80,48},{96,128},{112,80},... | collective-permute-start | bytes 2359304 | tf_op jit(solution)/shard_map/ppermute | solution.py:140
  43.1 0.7 reduce
  43.8 0.1 reshape.16
  43.9 0.8 copy.9
  44.7 0.1 reshape_squeeze.7
  44.8 0.7 fusion.1
  45.5 0.7 concatenate.6.scalar_ref
  46.2 0.0 copy-start
  46.2 0.1 constant_dynamic-update-slice_fusion.1
  46.3 8.2 %collective-permute-done = bf16[3072,128]{1,0:T(8,128)(2,1)S(1)} collective-permute-done((bf16[3072,128]{1,0:T(8,128)(2,1)S(1)}, bf16[3072,128]{1,0:T(8,128)(2,1)S(1)}, u32[]{:S(2)}, u32[]{:S(2)}) %collective-permute-start) | collective-permute-done | bytes 786464 | tf_op jit(solution)/shard_map/ppermute | solution.py:140
  54.5 0.1 constant_dynamic-update-slice_fusion
  54.6 1.9 %collective-permute-start.1 = (bf16[6144,128]{1,0:T(8,128)(2,1)S(1)}, bf16[6144,128]{1,0:T(8,128)(2,1)S(1)}, u32[]{:S(2)}, u32[]{:S(2)}) collective-permute-start(bf16[6144,128]{1,0:T(8,128)(2,1)S(1)} %constant_dynamic-update-slice_fusion), channel_id=1, source_target_pairs={{0,16},{16,0},{32,48},{48,32},{64,80},{80,64},{96,112},{112,96},{1... | collective-permute-start | bytes 4718600 | tf_op jit(solution)/shard_map/ppermute | solution.py:144
  56.5 3.4 %collective-permute-done.1 = bf16[6144,128]{1,0:T(8,128)(2,1)S(1)} collective-permute-done((bf16[6144,128]{1,0:T(8,128)(2,1)S(1)}, bf16[6144,128]{1,0:T(8,128)(2,1)S(1)}, u32[]{:S(2)}, u32[]{:S(2)}) %collective-permute-start.1) | collective-permute-done | bytes 1572896 | tf_op jit(solution)/shard_map/ppermute | solution.py:144
  59.9 0.0 copy-done
  59.9 2.4 %shard_map.77 = bf16[16,784,128]{2,1,0:T(8,128)(2,1)S(1)} custom-call(s32[185]{0:T(256)S(1)} %concatenate.6.scalar_ref, bf16[32,128,128]{2,1,0:T(8,128)(2,1)S(1)} %bitcast.27, bf16[16,3,128,128]{3,2,1,0:T(8,128)(2,1)S(1)} %bitcast.25, bf16[16,3,128,128]{3,2,1,0:T(8,128)(2,1)S(1)} %bitcast.26), custom_call_target="tpu_custom_call" | custom-call | tf_op jit(solution)/shard_map/pallas_call | solution.py:186
  62.3 26.6 %all_to_all.15.got_ref = bf16[16,784,128]{2,1,0:T(8,128)(2,1)S(1)} all-to-all(bf16[16,784,128]{2,1,0:T(8,128)(2,1)S(1)} %shard_map.77), channel_id=1, replica_groups={{0,4,8,12},{1,5,9,13},{2,6,10,14},{3,7,11,15},{16,17,18,19},{20,21,22,2..., dimensions={0} | all-to-all | bytes 6422528 | tf_op jit(solution)/shard_map/all_to_all | solution.py:121
  88.9 1.8 %shard_map.78 = bf16[32,128,128]{2,1,0:T(8,128)(2,1)S(1)} custom-call(bf16[16,784,128]{2,1,0:T(8,128)(2,1)S(1)} %all_to_all.15.got_ref), custom_call_target="tpu_custom_call" | custom-call | tf_op jit(solution)/shard_map/pallas_call | solution.py:202
  90.7 0.0 copy-start.1
  90.7 14.3 %all_to_all.16.got_ref = bf16[32,128,128]{2,1,0:T(8,128)(2,1)S(1)} all-to-all(bf16[32,128,128]{2,1,0:T(8,128)(2,1)S(1)} %shard_map.78), channel_id=1, replica_groups={{0,1,2,3},{4,5,6,7},{8,9,10,11},{12,13,14,15},{16,20,24,28},{17,21,25,2..., dimensions={0} | all-to-all | bytes 2097152 | tf_op jit(solution)/shard_map/all_to_all | solution.py:121
  105.0 0.0 copy-done.1
  105.0 1.7 %shard_map.79 = (bf16[8,128,128]{2,1,0:T(8,128)(2,1)}, bf16[32,128,128]{2,1,0:T(8,128)(2,1)S(1)}) custom-call(s32[185]{0:T(256)S(1)} %concatenate.6.scalar_ref, bf16[3,128,128]{2,1,0:T(8,128)(2,1)S(1)} %bitcast.29, bf16[32,128,128]{2,1,0:T(8,128)(2,1)S(1)} %all_to_all.16.got_ref), custom_call_target="tpu_custom_call" | custom-call | tf_op jit(solution)/shard_map/pallas_call | solution.py:216
  106.7 17.6 %all_to_all.17 = bf16[32,128,128]{2,1,0:T(8,128)(2,1)S(1)} all-to-all(bf16[32,128,128]{2,1,0:T(8,128)(2,1)S(1)} %get-tuple-element.9), channel_id=1, replica_groups=mesh['row'=32,'col'=16] {'col'}, dimensions={0} | all-to-all | bytes 2097152 | tf_op jit(solution)/shard_map/all_to_all | solution.py:227
  124.4 0.8 convert_reduce_fusion
  (1 shorter events, 0.0 us)
Async XLA Ops:
  39.4 15.1 %collective-permute-start = (bf16[3072,128]{1,0:T(8,128)(2,1)S(1)}, bf16[3072,128]{1,0:T(8,128)(2,1)S(1)}, u32[]{:S(2)}, u32[]{:S(2)}) collective-permute-start(bf16[3072,128]{1,0:T(8,128)(2,1)S(1)} %all_gather.3), channel_id=1, source_target_pairs={{0,32},{16,496},{32,64},{48,16},{64,96},{80,48},{96,128},{112,80},... | collective-permute-start | bytes 2359304 | tf_op jit(solution)/shard_map/ppermute | solution.py:140
  46.2 13.7 %copy-start = (bf16[1,1,32,128,128]{4,3,2,1,0:T(8,128)(2,1)S(1)}, bf16[1,1,32,128,128]{4,3,2,1,0:T(8,128)(2,1)}, u32[]{:S(2)}) copy-start(bf16[1,1,32,128,128]{4,3,2,1,0:T(8,128)(2,1)} %param.6) | copy-start | bytes 3145732
  54.6 5.3 %collective-permute-start.1 = (bf16[6144,128]{1,0:T(8,128)(2,1)S(1)}, bf16[6144,128]{1,0:T(8,128)(2,1)S(1)}, u32[]{:S(2)}, u32[]{:S(2)}) collective-permute-start(bf16[6144,128]{1,0:T(8,128)(2,1)S(1)} %constant_dynamic-update-slice_fusion), channel_id=1, source_target_pairs={{0,16},{16,0},{32,48},{48,32},{64,80},{80,64},{96,112},{112,96},{1... | collective-permute-start | bytes 4718600 | tf_op jit(solution)/shard_map/ppermute | solution.py:144
  90.7 14.3 %copy-start.1 = (bf16[1,3,128,128]{3,2,1,0:T(8,128)(2,1)S(1)}, bf16[1,3,128,128]{3,2,1,0:T(8,128)(2,1)}, u32[]{:S(2)}) copy-start(bf16[1,3,128,128]{3,2,1,0:T(8,128)(2,1)} %param.10) | copy-start | bytes 294916

commit v5 on v4

--- a/solution.py
+++ b/solution.py
@@ -24,23 +24,7 @@
 SPOT = 2 * KA + KA * KP
 
 
-def product_kernel(scalar_ref, tile_ref, *rest):
-    pieces = rest[: len(PIECES)]
-    outs, panel, tiles, order, count, sems, tile_sem = rest[len(PIECES) :]
-    tile_copy = pltpu.make_async_copy(tile_ref, tiles, tile_sem.at[0])
-    tile_copy.start()
-    copies = []
-    for number, (piece, (first, size)) in enumerate(zip(pieces, PIECES)):
-        for k in range(KP):
-            copies.append(
-                pltpu.make_async_copy(
-                    piece.at[:, k],
-                    panel.at[pl.ds(first, size), :, pl.ds(k * TILE, TILE)],
-                    sems.at[number * KP + k],
-                )
-            )
-    for copy in copies:
-        copy.start()
+def product_kernel(scalar_ref, tile_ref, own_ref, other_ref, outs, order, count):
     for owner in range(COLS):
         count[owner] = 0
     for t in range(KA):
@@ -49,21 +33,21 @@
         count[owner] = which + 1
         order[owner * PAIR + which] = t
     lane = lax.broadcasted_iota(jnp.int32, (MARK, TILE), 1)
-    tile_copy.wait()
-    for copy in copies:
-        copy.wait()
     flipped = scalar_ref[SPOT + KP * KAP]
     for place in range(COLS):
         owner = jnp.where(flipped == 0, place, place % SIDE * SIDE + place // SIDE)
         mark = jnp.zeros((MARK, TILE), jnp.float32)
         for which in range(PAIR):
             t = order[owner * PAIR + which]
-            product = jnp.dot(
-                tiles[t], panel[scalar_ref[t]], preferred_element_type=jnp.float32
-            ).astype(jnp.bfloat16)
+            spot = scalar_ref[t]
+            mine = spot < RINGS
+            shard = spot % RINGS
+            tile = tile_ref[t]
             for k in range(KP):
                 q = which * KP + k
-                outs[place, q * TILE : (q + 1) * TILE, :] = product[:, k * TILE : (k + 1) * TILE]
+                block = jnp.where(mine, own_ref[shard, k], other_ref[shard, k])
+                product = jnp.dot(tile, block, preferred_element_type=jnp.float32)
+                outs[place, q * TILE : (q + 1) * TILE, :] = product.astype(jnp.bfloat16)
                 value = scalar_ref[2 * KA + t * KP + k].astype(jnp.float32)
                 mark = jnp.where(lane == q, value, mark)
         outs[place, BODY:, :] = mark.astype(jnp.bfloat16)
@@ -128,9 +112,6 @@
     )
 
 
-PIECES = ((0, 16), (16, 16))
-
-
 def from_neighbour(array):
     pairs = [
         (2 * z + core, 2 * ((z + (1 if core == 0 else -1)) % RINGS) + core)
@@ -169,8 +150,6 @@
 def on_device(stiff_tiles, stiff_rows, stiff_cols, product_slot, prolong_tiles, coarse_dest):
     scalars = pl.BlockSpec(memory_space=pltpu.SMEM)
     vmem = pl.BlockSpec(memory_space=pltpu.VMEM)
-    hbm = pl.BlockSpec(memory_space=pltpu.HBM)
-    anywhere = pl.BlockSpec(memory_space=pl.ANY)
     params = pltpu.CompilerParams(vmem_limit_bytes=24 * 2**20)
     prolong = prolong_tiles[0]
     numbers = jnp.concatenate(
@@ -186,15 +165,11 @@
     sent = pl.pallas_call(
         product_kernel,
         out_shape=jax.ShapeDtypeStruct((COLS, BLOCK, TILE), jnp.bfloat16),
-        in_specs=[scalars, hbm] + [anywhere] * len(PIECES),
+        in_specs=[scalars, vmem, vmem, vmem],
         out_specs=vmem,
         scratch_shapes=[
-            pltpu.VMEM((ROWS, TILE, SHARD), jnp.bfloat16),
-            pltpu.VMEM((KA, TILE, TILE), jnp.bfloat16),
             pltpu.SMEM((KA,), jnp.int32),
             pltpu.SMEM((COLS,), jnp.int32),
-            pltpu.SemaphoreType.DMA((len(PIECES) * KP,)),
-            pltpu.SemaphoreType.DMA((1,)),
         ],
         compiler_params=pltpu.CompilerParams(vmem_limit_bytes=K1_MIB * 2**20),
     )(numbers, stiff_tiles[0, 0], *pieces)

time: 126 us -> 125 us (level)
  transfers between devices with their start and end apart: 2 -> 2, of which waited for: 2 -> 2; matrix products, arithmetic and copies ran while one was open for 2% -> 3% of each run, Pallas kernels for 0% -> 0%
where the time goes in v5:
time: 125 us
  blocking collectives  97.3 us (78%)
  waiting for transfers between devices  11.6 us (9%)
  starting transfers between devices  5.61 us (4%)
  Pallas kernels  5.32 us (4%)
  other arithmetic  2.19 us (2%)
  local copies, waits for them, and re-layouts  1.85 us (1%)
    all_to_all x2, blocking collectives, exchange_side(): lax.all_to_all(array, ('row', 'col'), split_axis=0, concat_axis=0, tiled=...  40.8 us
    all_gather x1, blocking collectives, gather_pieces(): lax.all_gather(prolong.reshape(SHARD, TILE), 'row', axis=0, tiled=True, a...  38.8 us
    all_to_all x1, blocking collectives, on_device(): lax.all_to_all(merged, 'col', split_axis=0, concat_axis=0, tiled=True)  17.6 us
    ppermute x1, waiting for transfers between devices, from_neighbour(): return lax.ppermute(array, 'row', pairs)  8.21 us
    ppermute x1, starting transfers between devices, from_neighbour(): return lax.ppermute(array, 'row', pairs)  3.69 us
    ppermute x1, waiting for transfers between devices, to_sibling(): return lax.ppermute(array, 'row', [(r, r ^ 1) for r in range(ROWS)])  3.38 us
  transfers between devices with their start and end apart: 2, of which 2 were waited for; matrix products, arithmetic and copies ran while one was open for 3% of the time, Pallas kernels for 0%

profile of v5, /device:TPU:8, one launch (start us, length us, event | category | flops | bytes accessed | tf_op | source)
XLA Modules:
  0.0 124.5 jit_solution(667389804383035172)
XLA Ops:
  0.6 38.8 %all_gather.3 = bf16[3072,128]{1,0:T(8,128)(2,1)S(1)} all-gather(bf16[384,128]{1,0:T(8,128)(2,1)} %bitcast.28), channel_id=1, replica_groups={{0,64,128,192,256,320,384,448},{16,80,144,208,272,336,400,464},{32,96,1..., dimensions={0}, use_global_device_ids=true | all-gather | bytes 884736 | tf_op jit(solution)/shard_map/all_gather | solution.py:130
  39.4 3.7 %collective-permute-start = (bf16[3072,128]{1,0:T(8,128)(2,1)S(1)}, bf16[3072,128]{1,0:T(8,128)(2,1)S(1)}, u32[]{:S(2)}, u32[]{:S(2)}) collective-permute-start(bf16[3072,128]{1,0:T(8,128)(2,1)S(1)} %all_gather.3), channel_id=1, source_target_pairs={{0,32},{16,496},{32,64},{48,16},{64,96},{80,48},{96,128},{112,80},... | collective-permute-start | bytes 2359304 | tf_op jit(solution)/shard_map/ppermute | solution.py:121
  43.1 0.7 reduce
  43.8 0.1 reshape.16
  43.9 0.8 copy.9
  44.7 0.1 reshape_squeeze.7
  44.8 0.7 fusion.1
  45.5 0.7 concatenate.6.scalar_ref
  46.2 0.0 copy-start
  46.2 0.1 constant_dynamic-update-slice_fusion.1
  46.3 8.2 %collective-permute-done = bf16[3072,128]{1,0:T(8,128)(2,1)S(1)} collective-permute-done((bf16[3072,128]{1,0:T(8,128)(2,1)S(1)}, bf16[3072,128]{1,0:T(8,128)(2,1)S(1)}, u32[]{:S(2)}, u32[]{:S(2)}) %collective-permute-start) | collective-permute-done | bytes 786464 | tf_op jit(solution)/shard_map/ppermute | solution.py:121
  54.5 0.1 constant_dynamic-update-slice_fusion
  54.6 1.9 %collective-permute-start.1 = (bf16[6144,128]{1,0:T(8,128)(2,1)S(1)}, bf16[6144,128]{1,0:T(8,128)(2,1)S(1)}, u32[]{:S(2)}, u32[]{:S(2)}) collective-permute-start(bf16[6144,128]{1,0:T(8,128)(2,1)S(1)} %constant_dynamic-update-slice_fusion), channel_id=1, source_target_pairs={{0,16},{16,0},{32,48},{48,32},{64,80},{80,64},{96,112},{112,96},{1... | collective-permute-start | bytes 4718600 | tf_op jit(solution)/shard_map/ppermute | solution.py:125
  56.5 3.4 %collective-permute-done.1 = bf16[6144,128]{1,0:T(8,128)(2,1)S(1)} collective-permute-done((bf16[6144,128]{1,0:T(8,128)(2,1)S(1)}, bf16[6144,128]{1,0:T(8,128)(2,1)S(1)}, u32[]{:S(2)}, u32[]{:S(2)}) %collective-permute-start.1) | collective-permute-done | bytes 1572896 | tf_op jit(solution)/shard_map/ppermute | solution.py:125
  59.9 0.0 copy-done
  59.9 1.8 %shard_map.77 = bf16[16,784,128]{2,1,0:T(8,128)(2,1)S(1)} custom-call(s32[185]{0:T(256)S(1)} %concatenate.6.scalar_ref, bf16[32,128,128]{2,1,0:T(8,128)(2,1)S(1)} %bitcast.27, bf16[16,3,128,128]{3,2,1,0:T(8,128)(2,1)S(1)} %bitcast.25, bf16[16,3,128,128]{3,2,1,0:T(8,128)(2,1)S(1)} %bitcast.26), custom_call_target="tpu_custom_call" | custom-call | tf_op jit(solution)/shard_map/pallas_call | solution.py:165
  61.7 26.6 %all_to_all.15.got_ref = bf16[16,784,128]{2,1,0:T(8,128)(2,1)S(1)} all-to-all(bf16[16,784,128]{2,1,0:T(8,128)(2,1)S(1)} %shard_map.77), channel_id=1, replica_groups={{0,4,8,12},{1,5,9,13},{2,6,10,14},{3,7,11,15},{16,17,18,19},{20,21,22,2..., dimensions={0} | all-to-all | bytes 6422528 | tf_op jit(solution)/shard_map/all_to_all | solution.py:105
  88.3 1.8 %shard_map.78 = bf16[32,128,128]{2,1,0:T(8,128)(2,1)S(1)} custom-call(bf16[16,784,128]{2,1,0:T(8,128)(2,1)S(1)} %all_to_all.15.got_ref), custom_call_target="tpu_custom_call" | custom-call | tf_op jit(solution)/shard_map/pallas_call | solution.py:177
  90.1 0.0 copy-start.1
  90.1 14.3 %all_to_all.16.got_ref = bf16[32,128,128]{2,1,0:T(8,128)(2,1)S(1)} all-to-all(bf16[32,128,128]{2,1,0:T(8,128)(2,1)S(1)} %shard_map.78), channel_id=1, replica_groups={{0,1,2,3},{4,5,6,7},{8,9,10,11},{12,13,14,15},{16,20,24,28},{17,21,25,2..., dimensions={0} | all-to-all | bytes 2097152 | tf_op jit(solution)/shard_map/all_to_all | solution.py:105
  104.4 0.0 copy-done.1
  104.4 1.7 %shard_map.79 = (bf16[8,128,128]{2,1,0:T(8,128)(2,1)}, bf16[32,128,128]{2,1,0:T(8,128)(2,1)S(1)}) custom-call(s32[185]{0:T(256)S(1)} %concatenate.6.scalar_ref, bf16[3,128,128]{2,1,0:T(8,128)(2,1)S(1)} %bitcast.29, bf16[32,128,128]{2,1,0:T(8,128)(2,1)S(1)} %all_to_all.16.got_ref), custom_call_target="tpu_custom_call" | custom-call | tf_op jit(solution)/shard_map/pallas_call | solution.py:191
  106.1 17.6 %all_to_all.17 = bf16[32,128,128]{2,1,0:T(8,128)(2,1)S(1)} all-to-all(bf16[32,128,128]{2,1,0:T(8,128)(2,1)S(1)} %get-tuple-element.9), channel_id=1, replica_groups=mesh['row'=32,'col'=16] {'col'}, dimensions={0} | all-to-all | bytes 2097152 | tf_op jit(solution)/shard_map/all_to_all | solution.py:202
  123.7 0.8 convert_reduce_fusion
  (1 shorter events, 0.0 us)
Async XLA Ops:
  39.4 15.1 %collective-permute-start = (bf16[3072,128]{1,0:T(8,128)(2,1)S(1)}, bf16[3072,128]{1,0:T(8,128)(2,1)S(1)}, u32[]{:S(2)}, u32[]{:S(2)}) collective-permute-start(bf16[3072,128]{1,0:T(8,128)(2,1)S(1)} %all_gather.3), channel_id=1, source_target_pairs={{0,32},{16,496},{32,64},{48,16},{64,96},{80,48},{96,128},{112,80},... | collective-permute-start | bytes 2359304 | tf_op jit(solution)/shard_map/ppermute | solution.py:121
  46.2 13.7 %copy-start = (bf16[1,1,32,128,128]{4,3,2,1,0:T(8,128)(2,1)S(1)}, bf16[1,1,32,128,128]{4,3,2,1,0:T(8,128)(2,1)}, u32[]{:S(2)}) copy-start(bf16[1,1,32,128,128]{4,3,2,1,0:T(8,128)(2,1)} %param.6) | copy-start | bytes 3145732
  54.6 5.3 %collective-permute-start.1 = (bf16[6144,128]{1,0:T(8,128)(2,1)S(1)}, bf16[6144,128]{1,0:T(8,128)(2,1)S(1)}, u32[]{:S(2)}, u32[]{:S(2)}) collective-permute-start(bf16[6144,128]{1,0:T(8,128)(2,1)S(1)} %constant_dynamic-update-slice_fusion), channel_id=1, source_target_pairs={{0,16},{16,0},{32,48},{48,32},{64,80},{80,64},{96,112},{112,96},{1... | collective-permute-start | bytes 4718600 | tf_op jit(solution)/shard_map/ppermute | solution.py:125
  90.1 14.3 %copy-start.1 = (bf16[1,3,128,128]{3,2,1,0:T(8,128)(2,1)S(1)}, bf16[1,3,128,128]{3,2,1,0:T(8,128)(2,1)}, u32[]{:S(2)}) copy-start(bf16[1,3,128,128]{3,2,1,0:T(8,128)(2,1)} %param.10) | copy-start | bytes 294916

commit v6 on v5

--- a/solution.py
+++ b/solution.py
@@ -72,6 +72,7 @@
 
 def coarse_kernel(scalar_ref, prolong_ref, got_ref, ap_ref, out_ref, merged):
     merged[...] = jnp.zeros_like(merged)
+    turned = [prolong_ref[k].astype(jnp.float32).T.astype(jnp.bfloat16) for k in range(KP)]
     for s in range(KAP):
         total = got_ref[s].astype(jnp.float32)
         for peer in range(1, SIDE):
@@ -79,9 +80,7 @@
         ap = total.astype(jnp.bfloat16)
         ap_ref[s] = ap
         for k in range(KP):
-            term = lax.dot_general(
-                prolong_ref[k], ap, (((0,), (0,)), ((), ())), preferred_element_type=jnp.float32
-            )
+            term = jnp.dot(turned[k], ap, preferred_element_type=jnp.float32)
             bucket = scalar_ref[SPOT + k * KAP + s]
             merged[bucket] = merged[bucket] + term
     out_ref[...] = merged[...].astype(jnp.bfloat16)

time: 125 us -> 125 us (level)
  no operation moved by 1% of the time
where the time goes in v6:
time: 125 us
  blocking collectives  97.3 us (78%)
  waiting for transfers between devices  11.6 us (9%)
  starting transfers between devices  5.61 us (4%)
  Pallas kernels  5.36 us (4%)
  other arithmetic  2.19 us (2%)
  local copies, waits for them, and re-layouts  1.85 us (1%)
    all_to_all x2, blocking collectives, exchange_side(): lax.all_to_all(array, ('row', 'col'), split_axis=0, concat_axis=0, tiled=...  40.8 us
    all_gather x1, blocking collectives, gather_pieces(): lax.all_gather(prolong.reshape(SHARD, TILE), 'row', axis=0, tiled=True, a...  38.8 us
    all_to_all x1, blocking collectives, on_device(): lax.all_to_all(merged, 'col', split_axis=0, concat_axis=0, tiled=True)  17.6 us
    ppermute x1, waiting for transfers between devices, from_neighbour(): return lax.ppermute(array, 'row', pairs)  8.21 us
    ppermute x1, starting transfers between devices, from_neighbour(): return lax.ppermute(array, 'row', pairs)  3.69 us
    ppermute x1, waiting for transfers between devices, to_sibling(): return lax.ppermute(array, 'row', [(r, r ^ 1) for r in range(ROWS)])  3.38 us
  transfers between devices with their start and end apart: 2, of which 2 were waited for; matrix products, arithmetic and copies ran while one was open for 3% of the time, Pallas kernels for 0%

profile of v6, /device:TPU:8, one launch (start us, length us, event | category | flops | bytes accessed | tf_op | source)
XLA Modules:
  0.0 124.6 jit_solution(949045906311188166)
XLA Ops:
  0.6 38.8 %all_gather.3 = bf16[3072,128]{1,0:T(8,128)(2,1)S(1)} all-gather(bf16[384,128]{1,0:T(8,128)(2,1)} %bitcast.28), channel_id=1, replica_groups={{0,64,128,192,256,320,384,448},{16,80,144,208,272,336,400,464},{32,96,1..., dimensions={0}, use_global_device_ids=true | all-gather | bytes 884736 | tf_op jit(solution)/shard_map/all_gather | solution.py:129
  39.4 3.7 %collective-permute-start = (bf16[3072,128]{1,0:T(8,128)(2,1)S(1)}, bf16[3072,128]{1,0:T(8,128)(2,1)S(1)}, u32[]{:S(2)}, u32[]{:S(2)}) collective-permute-start(bf16[3072,128]{1,0:T(8,128)(2,1)S(1)} %all_gather.3), channel_id=1, source_target_pairs={{0,32},{16,496},{32,64},{48,16},{64,96},{80,48},{96,128},{112,80},... | collective-permute-start | bytes 2359304 | tf_op jit(solution)/shard_map/ppermute | solution.py:120
  43.1 0.7 reduce
  43.8 0.1 reshape.16
  43.9 0.8 copy.9
  44.7 0.1 reshape_squeeze.7
  44.8 0.7 fusion.1
  45.5 0.7 concatenate.6.scalar_ref
  46.2 0.0 copy-start
  46.2 0.1 constant_dynamic-update-slice_fusion.1
  46.3 8.2 %collective-permute-done = bf16[3072,128]{1,0:T(8,128)(2,1)S(1)} collective-permute-done((bf16[3072,128]{1,0:T(8,128)(2,1)S(1)}, bf16[3072,128]{1,0:T(8,128)(2,1)S(1)}, u32[]{:S(2)}, u32[]{:S(2)}) %collective-permute-start) | collective-permute-done | bytes 786464 | tf_op jit(solution)/shard_map/ppermute | solution.py:120
  54.5 0.1 constant_dynamic-update-slice_fusion
  54.6 1.9 %collective-permute-start.1 = (bf16[6144,128]{1,0:T(8,128)(2,1)S(1)}, bf16[6144,128]{1,0:T(8,128)(2,1)S(1)}, u32[]{:S(2)}, u32[]{:S(2)}) collective-permute-start(bf16[6144,128]{1,0:T(8,128)(2,1)S(1)} %constant_dynamic-update-slice_fusion), channel_id=1, source_target_pairs={{0,16},{16,0},{32,48},{48,32},{64,80},{80,64},{96,112},{112,96},{1... | collective-permute-start | bytes 4718600 | tf_op jit(solution)/shard_map/ppermute | solution.py:124
  56.5 3.4 %collective-permute-done.1 = bf16[6144,128]{1,0:T(8,128)(2,1)S(1)} collective-permute-done((bf16[6144,128]{1,0:T(8,128)(2,1)S(1)}, bf16[6144,128]{1,0:T(8,128)(2,1)S(1)}, u32[]{:S(2)}, u32[]{:S(2)}) %collective-permute-start.1) | collective-permute-done | bytes 1572896 | tf_op jit(solution)/shard_map/ppermute | solution.py:124
  59.9 0.0 copy-done
  59.9 1.8 %shard_map.77 = bf16[16,784,128]{2,1,0:T(8,128)(2,1)S(1)} custom-call(s32[185]{0:T(256)S(1)} %concatenate.6.scalar_ref, bf16[32,128,128]{2,1,0:T(8,128)(2,1)S(1)} %bitcast.27, bf16[16,3,128,128]{3,2,1,0:T(8,128)(2,1)S(1)} %bitcast.25, bf16[16,3,128,128]{3,2,1,0:T(8,128)(2,1)S(1)} %bitcast.26), custom_call_target="tpu_custom_call" | custom-call | tf_op jit(solution)/shard_map/pallas_call | solution.py:164
  61.7 26.6 %all_to_all.15.got_ref = bf16[16,784,128]{2,1,0:T(8,128)(2,1)S(1)} all-to-all(bf16[16,784,128]{2,1,0:T(8,128)(2,1)S(1)} %shard_map.77), channel_id=1, replica_groups={{0,4,8,12},{1,5,9,13},{2,6,10,14},{3,7,11,15},{16,17,18,19},{20,21,22,2..., dimensions={0} | all-to-all | bytes 6422528 | tf_op jit(solution)/shard_map/all_to_all | solution.py:104
  88.3 1.8 %shard_map.78 = bf16[32,128,128]{2,1,0:T(8,128)(2,1)S(1)} custom-call(bf16[16,784,128]{2,1,0:T(8,128)(2,1)S(1)} %all_to_all.15.got_ref), custom_call_target="tpu_custom_call" | custom-call | tf_op jit(solution)/shard_map/pallas_call | solution.py:176
  90.1 0.0 copy-start.1
  90.1 14.3 %all_to_all.16.got_ref = bf16[32,128,128]{2,1,0:T(8,128)(2,1)S(1)} all-to-all(bf16[32,128,128]{2,1,0:T(8,128)(2,1)S(1)} %shard_map.78), channel_id=1, replica_groups={{0,1,2,3},{4,5,6,7},{8,9,10,11},{12,13,14,15},{16,20,24,28},{17,21,25,2..., dimensions={0} | all-to-all | bytes 2097152 | tf_op jit(solution)/shard_map/all_to_all | solution.py:104
  104.4 0.0 copy-done.1
  104.4 1.8 %shard_map.79 = (bf16[8,128,128]{2,1,0:T(8,128)(2,1)}, bf16[32,128,128]{2,1,0:T(8,128)(2,1)S(1)}) custom-call(s32[185]{0:T(256)S(1)} %concatenate.6.scalar_ref, bf16[3,128,128]{2,1,0:T(8,128)(2,1)S(1)} %bitcast.29, bf16[32,128,128]{2,1,0:T(8,128)(2,1)S(1)} %all_to_all.16.got_ref), custom_call_target="tpu_custom_call" | custom-call | tf_op jit(solution)/shard_map/pallas_call | solution.py:190
  106.2 17.6 %all_to_all.17 = bf16[32,128,128]{2,1,0:T(8,128)(2,1)S(1)} all-to-all(bf16[32,128,128]{2,1,0:T(8,128)(2,1)S(1)} %get-tuple-element.9), channel_id=1, replica_groups=mesh['row'=32,'col'=16] {'col'}, dimensions={0} | all-to-all | bytes 2097152 | tf_op jit(solution)/shard_map/all_to_all | solution.py:201
  123.8 0.8 convert_reduce_fusion
  (1 shorter events, 0.0 us)
Async XLA Ops:
  39.4 15.1 %collective-permute-start = (bf16[3072,128]{1,0:T(8,128)(2,1)S(1)}, bf16[3072,128]{1,0:T(8,128)(2,1)S(1)}, u32[]{:S(2)}, u32[]{:S(2)}) collective-permute-start(bf16[3072,128]{1,0:T(8,128)(2,1)S(1)} %all_gather.3), channel_id=1, source_target_pairs={{0,32},{16,496},{32,64},{48,16},{64,96},{80,48},{96,128},{112,80},... | collective-permute-start | bytes 2359304 | tf_op jit(solution)/shard_map/ppermute | solution.py:120
  46.2 13.7 %copy-start = (bf16[1,1,32,128,128]{4,3,2,1,0:T(8,128)(2,1)S(1)}, bf16[1,1,32,128,128]{4,3,2,1,0:T(8,128)(2,1)}, u32[]{:S(2)}) copy-start(bf16[1,1,32,128,128]{4,3,2,1,0:T(8,128)(2,1)} %param.6) | copy-start | bytes 3145732
  54.6 5.3 %collective-permute-start.1 = (bf16[6144,128]{1,0:T(8,128)(2,1)S(1)}, bf16[6144,128]{1,0:T(8,128)(2,1)S(1)}, u32[]{:S(2)}, u32[]{:S(2)}) collective-permute-start(bf16[6144,128]{1,0:T(8,128)(2,1)S(1)} %constant_dynamic-update-slice_fusion), channel_id=1, source_target_pairs={{0,16},{16,0},{32,48},{48,32},{64,80},{80,64},{96,112},{112,96},{1... | collective-permute-start | bytes 4718600 | tf_op jit(solution)/shard_map/ppermute | solution.py:124
  90.1 14.3 %copy-start.1 = (bf16[1,3,128,128]{3,2,1,0:T(8,128)(2,1)S(1)}, bf16[1,3,128,128]{3,2,1,0:T(8,128)(2,1)}, u32[]{:S(2)}) copy-start(bf16[1,3,128,128]{3,2,1,0:T(8,128)(2,1)} %param.10) | copy-start | bytes 294916

commit v7 on v6

--- a/solution.py
+++ b/solution.py
@@ -60,14 +60,15 @@
     scalar_copy.start()
     total[...] = jnp.zeros_like(total)
     scalar_copy.wait()
-    for peer in range(SIDE):
-        for owner in range(SIDE):
+    for owner in range(SIDE):
+        for peer in range(SIDE):
             block = peer * SIDE + owner
             for q in range(PAIR * KP):
                 where = owner * KAP + mark_scalar[block, q]
                 part = got_ref[block, q * TILE : (q + 1) * TILE, :]
                 total[where] = total[where] + part.astype(jnp.float32)
-    out_ref[...] = total[...].astype(jnp.bfloat16)
+        mine = slice(owner * KAP, (owner + 1) * KAP)
+        out_ref[mine] = total[mine].astype(jnp.bfloat16)
 
 
 def coarse_kernel(scalar_ref, prolong_ref, got_ref, ap_ref, out_ref, merged):

time: 125 us -> 125 us (level)
  no operation moved by 1% of the time
where the time goes in v7:
time: 125 us
  blocking collectives  97.2 us (78%)
  waiting for transfers between devices  11.6 us (9%)
  starting transfers between devices  5.61 us (4%)
  Pallas kernels  5.33 us (4%)
  other arithmetic  2.19 us (2%)
  local copies, waits for them, and re-layouts  1.85 us (1%)
    all_to_all x2, blocking collectives, exchange_side(): lax.all_to_all(array, ('row', 'col'), split_axis=0, concat_axis=0, tiled=...  40.8 us
    all_gather x1, blocking collectives, gather_pieces(): lax.all_gather(prolong.reshape(SHARD, TILE), 'row', axis=0, tiled=True, a...  38.8 us
    all_to_all x1, blocking collectives, on_device(): lax.all_to_all(merged, 'col', split_axis=0, concat_axis=0, tiled=True)  17.6 us
    ppermute x1, waiting for transfers between devices, from_neighbour(): return lax.ppermute(array, 'row', pairs)  8.21 us
    ppermute x1, starting transfers between devices, from_neighbour(): return lax.ppermute(array, 'row', pairs)  3.69 us
    ppermute x1, waiting for transfers between devices, to_sibling(): return lax.ppermute(array, 'row', [(r, r ^ 1) for r in range(ROWS)])  3.38 us
  transfers between devices with their start and end apart: 2, of which 2 were waited for; matrix products, arithmetic and copies ran while one was open for 3% of the time, Pallas kernels for 0%

profile of v7, /device:TPU:8, one launch (start us, length us, event | category | flops | bytes accessed | tf_op | source)
XLA Modules:
  0.0 124.5 jit_solution(13337340761914176249)
XLA Ops:
  0.6 38.8 %all_gather.3 = bf16[3072,128]{1,0:T(8,128)(2,1)S(1)} all-gather(bf16[384,128]{1,0:T(8,128)(2,1)} %bitcast.28), channel_id=1, replica_groups={{0,64,128,192,256,320,384,448},{16,80,144,208,272,336,400,464},{32,96,1..., dimensions={0}, use_global_device_ids=true | all-gather | bytes 884736 | tf_op jit(solution)/shard_map/all_gather | solution.py:130
  39.4 3.7 %collective-permute-start = (bf16[3072,128]{1,0:T(8,128)(2,1)S(1)}, bf16[3072,128]{1,0:T(8,128)(2,1)S(1)}, u32[]{:S(2)}, u32[]{:S(2)}) collective-permute-start(bf16[3072,128]{1,0:T(8,128)(2,1)S(1)} %all_gather.3), channel_id=1, source_target_pairs={{0,32},{16,496},{32,64},{48,16},{64,96},{80,48},{96,128},{112,80},... | collective-permute-start | bytes 2359304 | tf_op jit(solution)/shard_map/ppermute | solution.py:121
  43.1 0.7 reduce
  43.8 0.1 reshape.16
  43.9 0.8 copy.9
  44.7 0.1 reshape_squeeze.7
  44.8 0.7 fusion.1
  45.5 0.7 concatenate.6.scalar_ref
  46.2 0.0 copy-start
  46.2 0.1 constant_dynamic-update-slice_fusion.1
  46.3 8.2 %collective-permute-done = bf16[3072,128]{1,0:T(8,128)(2,1)S(1)} collective-permute-done((bf16[3072,128]{1,0:T(8,128)(2,1)S(1)}, bf16[3072,128]{1,0:T(8,128)(2,1)S(1)}, u32[]{:S(2)}, u32[]{:S(2)}) %collective-permute-start) | collective-permute-done | bytes 786464 | tf_op jit(solution)/shard_map/ppermute | solution.py:121
  54.5 0.1 constant_dynamic-update-slice_fusion
  54.6 1.9 %collective-permute-start.1 = (bf16[6144,128]{1,0:T(8,128)(2,1)S(1)}, bf16[6144,128]{1,0:T(8,128)(2,1)S(1)}, u32[]{:S(2)}, u32[]{:S(2)}) collective-permute-start(bf16[6144,128]{1,0:T(8,128)(2,1)S(1)} %constant_dynamic-update-slice_fusion), channel_id=1, source_target_pairs={{0,16},{16,0},{32,48},{48,32},{64,80},{80,64},{96,112},{112,96},{1... | collective-permute-start | bytes 4718600 | tf_op jit(solution)/shard_map/ppermute | solution.py:125
  56.5 3.4 %collective-permute-done.1 = bf16[6144,128]{1,0:T(8,128)(2,1)S(1)} collective-permute-done((bf16[6144,128]{1,0:T(8,128)(2,1)S(1)}, bf16[6144,128]{1,0:T(8,128)(2,1)S(1)}, u32[]{:S(2)}, u32[]{:S(2)}) %collective-permute-start.1) | collective-permute-done | bytes 1572896 | tf_op jit(solution)/shard_map/ppermute | solution.py:125
  59.9 0.0 copy-done
  59.9 1.8 %shard_map.77 = bf16[16,784,128]{2,1,0:T(8,128)(2,1)S(1)} custom-call(s32[185]{0:T(256)S(1)} %concatenate.6.scalar_ref, bf16[32,128,128]{2,1,0:T(8,128)(2,1)S(1)} %bitcast.27, bf16[16,3,128,128]{3,2,1,0:T(8,128)(2,1)S(1)} %bitcast.25, bf16[16,3,128,128]{3,2,1,0:T(8,128)(2,1)S(1)} %bitcast.26), custom_call_target="tpu_custom_call" | custom-call | tf_op jit(solution)/shard_map/pallas_call | solution.py:165
  61.7 26.6 %all_to_all.15.got_ref = bf16[16,784,128]{2,1,0:T(8,128)(2,1)S(1)} all-to-all(bf16[16,784,128]{2,1,0:T(8,128)(2,1)S(1)} %shard_map.77), channel_id=1, replica_groups={{0,4,8,12},{1,5,9,13},{2,6,10,14},{3,7,11,15},{16,17,18,19},{20,21,22,2..., dimensions={0} | all-to-all | bytes 6422528 | tf_op jit(solution)/shard_map/all_to_all | solution.py:105
  88.3 1.8 %shard_map.78 = bf16[32,128,128]{2,1,0:T(8,128)(2,1)S(1)} custom-call(bf16[16,784,128]{2,1,0:T(8,128)(2,1)S(1)} %all_to_all.15.got_ref), custom_call_target="tpu_custom_call" | custom-call | tf_op jit(solution)/shard_map/pallas_call | solution.py:177
  90.1 0.0 copy-start.1
  90.1 14.3 %all_to_all.16.got_ref = bf16[32,128,128]{2,1,0:T(8,128)(2,1)S(1)} all-to-all(bf16[32,128,128]{2,1,0:T(8,128)(2,1)S(1)} %shard_map.78), channel_id=1, replica_groups={{0,1,2,3},{4,5,6,7},{8,9,10,11},{12,13,14,15},{16,20,24,28},{17,21,25,2..., dimensions={0} | all-to-all | bytes 2097152 | tf_op jit(solution)/shard_map/all_to_all | solution.py:105
  104.4 0.0 copy-done.1
  104.4 1.8 %shard_map.79 = (bf16[8,128,128]{2,1,0:T(8,128)(2,1)}, bf16[32,128,128]{2,1,0:T(8,128)(2,1)S(1)}) custom-call(s32[185]{0:T(256)S(1)} %concatenate.6.scalar_ref, bf16[3,128,128]{2,1,0:T(8,128)(2,1)S(1)} %bitcast.29, bf16[32,128,128]{2,1,0:T(8,128)(2,1)S(1)} %all_to_all.16.got_ref), custom_call_target="tpu_custom_call" | custom-call | tf_op jit(solution)/shard_map/pallas_call | solution.py:191
  106.1 17.6 %all_to_all.17 = bf16[32,128,128]{2,1,0:T(8,128)(2,1)S(1)} all-to-all(bf16[32,128,128]{2,1,0:T(8,128)(2,1)S(1)} %get-tuple-element.9), channel_id=1, replica_groups=mesh['row'=32,'col'=16] {'col'}, dimensions={0} | all-to-all | bytes 2097152 | tf_op jit(solution)/shard_map/all_to_all | solution.py:202
  123.7 0.8 convert_reduce_fusion
  (1 shorter events, 0.0 us)
Async XLA Ops:
  39.4 15.1 %collective-permute-start = (bf16[3072,128]{1,0:T(8,128)(2,1)S(1)}, bf16[3072,128]{1,0:T(8,128)(2,1)S(1)}, u32[]{:S(2)}, u32[]{:S(2)}) collective-permute-start(bf16[3072,128]{1,0:T(8,128)(2,1)S(1)} %all_gather.3), channel_id=1, source_target_pairs={{0,32},{16,496},{32,64},{48,16},{64,96},{80,48},{96,128},{112,80},... | collective-permute-start | bytes 2359304 | tf_op jit(solution)/shard_map/ppermute | solution.py:121
  46.2 13.7 %copy-start = (bf16[1,1,32,128,128]{4,3,2,1,0:T(8,128)(2,1)S(1)}, bf16[1,1,32,128,128]{4,3,2,1,0:T(8,128)(2,1)}, u32[]{:S(2)}) copy-start(bf16[1,1,32,128,128]{4,3,2,1,0:T(8,128)(2,1)} %param.6) | copy-start | bytes 3145732
  54.6 5.3 %collective-permute-start.1 = (bf16[6144,128]{1,0:T(8,128)(2,1)S(1)}, bf16[6144,128]{1,0:T(8,128)(2,1)S(1)}, u32[]{:S(2)}, u32[]{:S(2)}) collective-permute-start(bf16[6144,128]{1,0:T(8,128)(2,1)S(1)} %constant_dynamic-update-slice_fusion), channel_id=1, source_target_pairs={{0,16},{16,0},{32,48},{48,32},{64,80},{80,64},{96,112},{112,96},{1... | collective-permute-start | bytes 4718600 | tf_op jit(solution)/shard_map/ppermute | solution.py:125
  90.1 14.3 %copy-start.1 = (bf16[1,3,128,128]{3,2,1,0:T(8,128)(2,1)S(1)}, bf16[1,3,128,128]{3,2,1,0:T(8,128)(2,1)}, u32[]{:S(2)}) copy-start(bf16[1,3,128,128]{3,2,1,0:T(8,128)(2,1)} %param.10) | copy-start | bytes 294916
